TPU v7x, 128 devices: a whole 4x4x4 slice. The times are simulated.
128 devices in a mesh: ctx: 8 (over y, z_hi), fsdp: 16 (over x, z_lo, core).
Axes of the slice: x: 4, y: 4, z: 4 (z_hi: 2, z_lo: 2; z = z_hi * 2 + z_lo), core: 2. Of those that a mesh axis runs over, the one named last changes fastest.
Arguments:
- tokens: bfloat16 [16384, 1280], P(('ctx', 'fsdp')), may hold values from -6 to 6
- norm_gain: bfloat16 [1280], P(('ctx', 'fsdp')), may hold values from 0.099609375 to 1.8984375
- w_query: bfloat16 [1280, 1280], P(('ctx', 'fsdp')), may hold values from -0.25 to 0.25
- w_key: bfloat16 [1280, 320], P(('ctx', 'fsdp')), may hold values from -0.15625 to 0.15625
- w_value: bfloat16 [1280, 320], P(('ctx', 'fsdp')), may hold values from -0.15625 to 0.15625
- w_out: bfloat16 [1280, 1280], P(('ctx', 'fsdp')), may hold values from -0.625 to 0.625
- mlp_gain: bfloat16 [1280], P(('ctx', 'fsdp')), may hold values from 0.099609375 to 1.8984375
- w_gate: bfloat16 [1280, 3584], P(('ctx', 'fsdp')), may hold values from -0.15625 to 0.15625
- w_up: bfloat16 [1280, 3584], P(('ctx', 'fsdp')), may hold values from -0.15625 to 0.15625
- w_down: bfloat16 [3584, 1280], P(('ctx', 'fsdp')), may hold values from -0.09375 to 0.09375
- block_pair: int32 [16, 8], P('fsdp'), may hold values from 0 to 7, each once within a row
- seq_len: int32 [16], P('fsdp'), may hold values from 640 to 1024, as said below
- seq_start: int32 [16], P('fsdp'), may hold values from 0 to 63, as said below
- out_grad: bfloat16 [16384, 1280], P(('ctx', 'fsdp')), may hold values from -6 to 6
Outputs:
- activations: bfloat16 [16384, 1280], P(('ctx', 'fsdp'))
- input_grad: bfloat16 [16384, 1280], P(('ctx', 'fsdp'))
- grad_norm_gain: float32 [1280], P(('ctx', 'fsdp'))
- grad_query: float32 [1280, 1280], P(('ctx', 'fsdp'))
- grad_key: float32 [1280, 320], P(('ctx', 'fsdp'))
- grad_value: float32 [1280, 320], P(('ctx', 'fsdp'))
- grad_out: float32 [1280, 1280], P(('ctx', 'fsdp'))
- grad_mlp_gain: float32 [1280], P(('ctx', 'fsdp'))
- grad_gate: float32 [1280, 3584], P(('ctx', 'fsdp'))
- grad_up: float32 [1280, 3584], P(('ctx', 'fsdp'))
- grad_down: float32 [3584, 1280], P(('ctx', 'fsdp'))
- seq_rms: float32 [16, 3], P('fsdp')
Inputs may be any that keep to these rules, and one draw needn't show every extreme that they name: The one sequence of group g fills slots seq_start[g] to seq_start[g] + seq_len[g] - 1 of the group's 1024 slots; some group fills all of them. seq_start[g] + seq_len[g] <= 1024.
All inputs are finite; a program needn't handle non-finite values.
Results may differ from a plain program's by a relative error of at most 0.022.
Values may be sent and summed in bfloat16 or wider, within the bound.
No kernel may reach another device: no remote copies, remote signals or barrier semaphores. Data moves between devices by JAX's collectives and lax.ppermute only.
A program may use at most 128 MiB of HBM per device.

v0:
```python
import jax
import jax.numpy as jnp
from jax import lax
from jax.sharding import PartitionSpec as P

QUERY_HEADS = 20
KEY_VALUE_HEADS = 5
HEAD_WIDTH = 64


EPSILON = 1e-05
ROPE_BASE = 10000.0
MASKED_SCORE = -1e30


def norm_apply(values, gain_values):
    factor = lax.rsqrt(jnp.mean(values * values, axis=-1, keepdims=True) + EPSILON)
    return values * factor * gain_values


def swiglu(gate_part, up_part):
    return jax.nn.silu(gate_part) * up_part


def rope_tables(angles_at, head_size):
    half_size = head_size // 2
    powers = jnp.arange(half_size, dtype=jnp.float32) * (2.0 / head_size)
    speeds = jnp.power(ROPE_BASE, -powers)
    angles = angles_at[:, None] * speeds[None, :]
    return (jnp.cos(angles)[:, None, :], jnp.sin(angles)[:, None, :])


def apply_rotary(values, cosine_values, sine_values):
    half_size = values.shape[-1] // 2
    leading = values[..., :half_size]
    trailing = values[..., half_size:]
    return jnp.concatenate(
        [
            leading * cosine_values - trailing * sine_values,
            trailing * cosine_values + leading * sine_values,
        ],
        axis=-1,
    )


def group_places(pair_row, devices_ctx, block_size):
    slots = jnp.arange(devices_ctx * 2 * block_size, dtype=jnp.int32)
    owners = slots // (2 * block_size)
    inside = slots % (2 * block_size)
    columns = jnp.arange(devices_ctx, dtype=jnp.int32)
    paired = jnp.sum(jnp.where(owners[:, None] == columns[None, :], pair_row[None, :], 0), axis=1)
    blocks = jnp.where(inside < block_size, paired, 2 * devices_ctx - 1 - paired)
    return blocks * block_size + inside % block_size


def head_scores(query_head, key_head, allowed, scale_factor):
    scores = (
        jnp.einsum("grd,kd->grk", query_head, key_head, preferred_element_type=jnp.float32)
        * scale_factor
    )
    return jnp.where(allowed[None], scores, MASKED_SCORE)


def head_forward(query_head, key_head, value_head, allowed, scale_factor):
    scores = head_scores(query_head, key_head, allowed, scale_factor)
    row_top = jnp.max(scores, axis=-1, keepdims=True)
    expons = jnp.exp(scores - row_top)
    totals = jnp.sum(expons, axis=-1, keepdims=True)
    chances = (expons / totals).astype(jnp.bfloat16)
    outcome = jnp.einsum("grk,kd->grd", chances, value_head, preferred_element_type=jnp.float32)
    return (outcome, row_top[..., 0] + jnp.log(totals[..., 0]))


def head_backward(query_head, key_head, value_head, grad_head, log_totals, allowed, scale_factor):
    scores = head_scores(query_head, key_head, allowed, scale_factor)
    chances = jnp.exp(scores - log_totals[..., None])
    chances_low = chances.astype(jnp.bfloat16)
    chance_grad = jnp.einsum(
        "grd,kd->grk", grad_head, value_head, preferred_element_type=jnp.float32
    )
    weighted = jnp.sum(chances * chance_grad, axis=-1, keepdims=True)
    score_grad = (chances * (chance_grad - weighted)).astype(jnp.bfloat16)
    query_grad = (
        jnp.einsum("grk,kd->grd", score_grad, key_head, preferred_element_type=jnp.float32)
        * scale_factor
    )
    key_grad = (
        jnp.einsum("grk,grd->kd", score_grad, query_head, preferred_element_type=jnp.float32)
        * scale_factor
    )
    value_grad = jnp.einsum(
        "grk,grd->kd", chances_low, grad_head, preferred_element_type=jnp.float32
    )
    return (query_grad, key_grad, value_grad)


def local(
    tokens,
    norm_gain,
    w_query,
    w_key,
    w_value,
    w_out,
    mlp_gain,
    w_gate,
    w_up,
    w_down,
    block_pair,
    seq_len,
    seq_start,
    out_grad,
):
    shard_rows = tokens.shape[0]
    block_size = shard_rows // 2
    model_width = tokens.shape[1]
    devices_ctx = lax.axis_size("ctx")
    position = lax.axis_index("ctx")
    query_per_key_ratio = QUERY_HEADS // KEY_VALUE_HEADS
    scale_factor = HEAD_WIDTH ** (-0.5)
    places_all = group_places(block_pair[0], devices_ctx, block_size)
    places_here = lax.dynamic_slice_in_dim(places_all, position * shard_rows, shard_rows)
    first_slot = seq_start[0]
    seq_length = seq_len[0]
    valid_all = (places_all >= first_slot) & (places_all < first_slot + seq_length)
    valid_here = (places_here >= first_slot) & (places_here < first_slot + seq_length)
    allowed = valid_here[:, None] & valid_all[None, :] & (
        places_all[None, :] <= places_here[:, None]
    ) | (places_all[None, :] == places_here[:, None])
    cosine_lookup, sine_lookup = rope_tables(
        (places_here - first_slot).astype(jnp.float32), HEAD_WIDTH
    )
    gain_one, gain_two, query_full, key_full, value_full, out_full = (
        lax.all_gather(norm_gain, ("ctx", "fsdp"), axis=0, tiled=True),
        lax.all_gather(mlp_gain, ("ctx", "fsdp"), axis=0, tiled=True),
        lax.all_gather(w_query, ("ctx", "fsdp"), axis=0, tiled=True),
        lax.all_gather(w_key, ("ctx", "fsdp"), axis=0, tiled=True),
        lax.all_gather(w_value, ("ctx", "fsdp"), axis=0, tiled=True),
        lax.all_gather(w_out, ("ctx", "fsdp"), axis=0, tiled=True),
    )
    inputs = tokens.astype(jnp.float32)
    gain_one_f = gain_one.astype(jnp.float32)
    normalized_rows = norm_apply(inputs, gain_one_f).astype(jnp.bfloat16)
    query_pre = jnp.dot(normalized_rows, query_full, preferred_element_type=jnp.float32)
    key_unrotated = jnp.dot(normalized_rows, key_full, preferred_element_type=jnp.float32)
    value_pre = jnp.dot(normalized_rows, value_full, preferred_element_type=jnp.float32)
    query_rotated = apply_rotary(
        query_pre.reshape(shard_rows, QUERY_HEADS, HEAD_WIDTH), cosine_lookup, sine_lookup
    ).astype(jnp.bfloat16)
    key_rotated = (
        apply_rotary(
            key_unrotated.reshape(shard_rows, KEY_VALUE_HEADS, HEAD_WIDTH),
            cosine_lookup,
            sine_lookup,
        )
        .astype(jnp.bfloat16)
        .reshape(shard_rows, KEY_VALUE_HEADS * HEAD_WIDTH)
    )
    value_reduced = value_pre.astype(jnp.bfloat16)
    gathered_keys, gathered_values = (
        lax.all_gather(key_rotated, "ctx", axis=0, tiled=True),
        lax.all_gather(value_reduced, "ctx", axis=0, tiled=True),
    )
    query_head_rows = query_rotated.reshape(
        shard_rows, KEY_VALUE_HEADS, query_per_key_ratio, HEAD_WIDTH
    ).transpose(1, 2, 0, 3)
    key_head_rows = gathered_keys.reshape(-1, KEY_VALUE_HEADS, HEAD_WIDTH).transpose(1, 0, 2)
    value_head_rows = gathered_values.reshape(-1, KEY_VALUE_HEADS, HEAD_WIDTH).transpose(1, 0, 2)

    def forward_head(pieces):
        return head_forward(pieces[0], pieces[1], pieces[2], allowed, scale_factor)

    head_outs, log_totals = lax.map(forward_head, (query_head_rows, key_head_rows, value_head_rows))
    attended = (
        head_outs.transpose(2, 0, 1, 3)
        .reshape(shard_rows, QUERY_HEADS * HEAD_WIDTH)
        .astype(jnp.bfloat16)
    )
    branch = jnp.dot(attended, out_full, preferred_element_type=jnp.float32)
    middle = inputs + branch
    gain_two_f = gain_two.astype(jnp.float32)
    normed_two = norm_apply(middle, gain_two_f).astype(jnp.bfloat16)
    gate_rows, up_rows, down_part = (
        lax.all_gather(w_gate, "fsdp", axis=0, tiled=True),
        lax.all_gather(w_up, "fsdp", axis=0, tiled=True),
        lax.all_gather(w_down, "fsdp", axis=0, tiled=True),
    )
    gate_part, up_part = (
        lax.all_to_all(gate_rows, "ctx", split_axis=1, concat_axis=0, tiled=True),
        lax.all_to_all(up_rows, "ctx", split_axis=1, concat_axis=0, tiled=True),
    )
    normed_rows = lax.all_gather(normed_two, "ctx", axis=0, tiled=True)
    gate_value = jnp.dot(normed_rows, gate_part, preferred_element_type=jnp.float32)
    up_value = jnp.dot(normed_rows, up_part, preferred_element_type=jnp.float32)
    hidden = swiglu(gate_value, up_value).astype(jnp.bfloat16)
    feed_out = lax.psum_scatter(
        jnp.dot(hidden, down_part, preferred_element_type=jnp.float32).astype(jnp.bfloat16),
        "ctx",
        scatter_dimension=0,
        tiled=True,
    ).astype(jnp.float32)
    final_out = middle + feed_out
    row_weight = valid_here.astype(jnp.float32)[:, None]
    local_sums = jnp.stack(
        [
            jnp.sum(row_weight * branch * branch),
            jnp.sum(row_weight * feed_out * feed_out),
            jnp.sum(row_weight * final_out * final_out),
        ]
    )
    global_sums = lax.psum(local_sums, "ctx")
    seq_rms = jnp.sqrt(global_sums / (seq_length.astype(jnp.float32) * model_width))[None, :]
    cotangent = out_grad.astype(jnp.float32) * row_weight
    feed_grad = cotangent.astype(jnp.bfloat16)
    swiglu_back = jax.vjp(swiglu, gate_value, up_value)[1]
    grad_rows = lax.all_gather(feed_grad, "ctx", axis=0, tiled=True)
    down_term = jnp.einsum("rf,rd->fd", hidden, grad_rows, preferred_element_type=jnp.float32)
    hidden_grad = jnp.einsum("rd,fd->rf", grad_rows, down_part, preferred_element_type=jnp.float32)
    gate_grad, up_grad = swiglu_back(hidden_grad)
    gate_low = gate_grad.astype(jnp.bfloat16)
    up_low = up_grad.astype(jnp.bfloat16)
    gate_term = jnp.einsum("rd,rf->df", normed_rows, gate_low, preferred_element_type=jnp.float32)
    up_term = jnp.einsum("rd,rf->df", normed_rows, up_low, preferred_element_type=jnp.float32)
    normed_two_grad = lax.psum_scatter(
        (
            jnp.einsum("rf,df->rd", gate_low, gate_part, preferred_element_type=jnp.float32)
            + jnp.einsum("rf,df->rd", up_low, up_part, preferred_element_type=jnp.float32)
        ).astype(jnp.bfloat16),
        "ctx",
        scatter_dimension=0,
        tiled=True,
    ).astype(jnp.float32)
    gate_cross, up_cross = (
        lax.all_to_all(
            gate_term.astype(jnp.bfloat16), "ctx", split_axis=0, concat_axis=1, tiled=True
        ).astype(gate_term.dtype),
        lax.all_to_all(
            up_term.astype(jnp.bfloat16), "ctx", split_axis=0, concat_axis=1, tiled=True
        ).astype(up_term.dtype),
    )
    gate_sum, up_sum, down_sum = (
        lax.psum_scatter(
            gate_cross.astype(jnp.bfloat16), "fsdp", scatter_dimension=0, tiled=True
        ).astype(jnp.float32),
        lax.psum_scatter(
            up_cross.astype(jnp.bfloat16), "fsdp", scatter_dimension=0, tiled=True
        ).astype(jnp.float32),
        lax.psum_scatter(
            down_term.astype(jnp.bfloat16), "fsdp", scatter_dimension=0, tiled=True
        ).astype(jnp.float32),
    )
    norm_two_back = jax.vjp(norm_apply, middle, gain_two_f)[1]
    middle_part, gain_two_term = norm_two_back(normed_two_grad)
    mid_grad = cotangent + middle_part
    query_back, key_back, value_back, out_back = (query_full, key_full, value_full, out_full)
    branch_grad = mid_grad.astype(jnp.bfloat16)
    out_term = jnp.einsum("rq,rd->qd", attended, branch_grad, preferred_element_type=jnp.float32)
    attended_gradient = jnp.einsum(
        "rd,qd->rq", branch_grad, out_back, preferred_element_type=jnp.float32
    ).astype(jnp.bfloat16)
    head_gradients = attended_gradient.reshape(
        shard_rows, KEY_VALUE_HEADS, query_per_key_ratio, HEAD_WIDTH
    ).transpose(1, 2, 0, 3)

    def backward_head(pieces):
        return head_backward(
            pieces[0], pieces[1], pieces[2], pieces[3], pieces[4], allowed, scale_factor
        )

    query_parts, key_pieces_list, value_pieces_list = lax.map(
        backward_head, (query_head_rows, key_head_rows, value_head_rows, head_gradients, log_totals)
    )
    query_grad_rot = query_parts.transpose(2, 0, 1, 3).reshape(shard_rows, QUERY_HEADS, HEAD_WIDTH)
    grouped_keys = key_pieces_list.transpose(1, 0, 2).reshape(-1, KEY_VALUE_HEADS * HEAD_WIDTH)
    grouped_values = value_pieces_list.transpose(1, 0, 2).reshape(-1, KEY_VALUE_HEADS * HEAD_WIDTH)
    local_keys, value_own = (
        lax.psum_scatter(
            grouped_keys.astype(jnp.bfloat16), "ctx", scatter_dimension=0, tiled=True
        ).astype(jnp.float32),
        lax.psum_scatter(
            grouped_values.astype(jnp.bfloat16), "ctx", scatter_dimension=0, tiled=True
        ).astype(jnp.float32),
    )
    query_low = (
        apply_rotary(query_grad_rot, cosine_lookup, -sine_lookup)
        .reshape(shard_rows, QUERY_HEADS * HEAD_WIDTH)
        .astype(jnp.bfloat16)
    )
    key_low = (
        apply_rotary(
            local_keys.reshape(shard_rows, KEY_VALUE_HEADS, HEAD_WIDTH), cosine_lookup, -sine_lookup
        )
        .reshape(shard_rows, KEY_VALUE_HEADS * HEAD_WIDTH)
        .astype(jnp.bfloat16)
    )
    value_grad_low = value_own.astype(jnp.bfloat16)
    query_term = jnp.einsum(
        "rd,rq->dq", normalized_rows, query_low, preferred_element_type=jnp.float32
    )
    key_term = jnp.einsum("rd,rk->dk", normalized_rows, key_low, preferred_element_type=jnp.float32)
    value_term = jnp.einsum(
        "rd,rk->dk", normalized_rows, value_grad_low, preferred_element_type=jnp.float32
    )
    normed_grad = jnp.einsum("rq,dq->rd", query_low, query_back, preferred_element_type=jnp.float32)
    normed_grad = normed_grad + jnp.einsum(
        "rk,dk->rd", key_low, key_back, preferred_element_type=jnp.float32
    )
    normed_grad = normed_grad + jnp.einsum(
        "rk,dk->rd", value_grad_low, value_back, preferred_element_type=jnp.float32
    )
    norm_one_back = jax.vjp(norm_apply, inputs, gain_one_f)[1]
    input_part, gain_one_term = norm_one_back(normed_grad)
    input_grad = (mid_grad + input_part).astype(jnp.bfloat16)
    gain_one_sum, gain_two_sum, query_sum, key_sum, value_sum, out_sum = (
        lax.psum_scatter(gain_one_term, ("ctx", "fsdp"), scatter_dimension=0, tiled=True),
        lax.psum_scatter(gain_two_term, ("ctx", "fsdp"), scatter_dimension=0, tiled=True),
        lax.psum_scatter(query_term, ("ctx", "fsdp"), scatter_dimension=0, tiled=True),
        lax.psum_scatter(key_term, ("ctx", "fsdp"), scatter_dimension=0, tiled=True),
        lax.psum_scatter(value_term, ("ctx", "fsdp"), scatter_dimension=0, tiled=True),
        lax.psum_scatter(out_term, ("ctx", "fsdp"), scatter_dimension=0, tiled=True),
    )
    return (
        final_out.astype(jnp.bfloat16),
        input_grad,
        gain_one_sum,
        query_sum,
        key_sum,
        value_sum,
        out_sum,
        gain_two_sum,
        gate_sum,
        up_sum,
        down_sum,
        seq_rms,
    )


def solution(mesh):
    in_specs = (
        P(("ctx", "fsdp"), None),
        P(("ctx", "fsdp")),
        P(("ctx", "fsdp"), None),
        P(("ctx", "fsdp"), None),
        P(("ctx", "fsdp"), None),
        P(("ctx", "fsdp"), None),
        P(("ctx", "fsdp")),
        P(("ctx", "fsdp"), None),
        P(("ctx", "fsdp"), None),
        P(("ctx", "fsdp"), None),
        P("fsdp", None),
        P("fsdp"),
        P("fsdp"),
        P(("ctx", "fsdp"), None),
    )
    out_specs = (
        P(("ctx", "fsdp"), None),
        P(("ctx", "fsdp"), None),
        P(("ctx", "fsdp")),
        P(("ctx", "fsdp"), None),
        P(("ctx", "fsdp"), None),
        P(("ctx", "fsdp"), None),
        P(("ctx", "fsdp"), None),
        P(("ctx", "fsdp")),
        P(("ctx", "fsdp"), None),
        P(("ctx", "fsdp"), None),
        P(("ctx", "fsdp"), None),
        P("fsdp", None),
    )
    return jax.shard_map(local, mesh=mesh, in_specs=in_specs, out_specs=out_specs, check_vma=False)
```

profile of v0, /device:TPU:1, one launch (start us, length us, event | category | flops | bytes accessed | tf_op | source)
XLA Modules:
  0.0 1433.7 jit_solution(3591863581758755090)
XLA Ops:
  14.9 68.9 %all-reduce.14 = (bf16[1280]{0:T(1024)(128)(2,1)S(1)}, bf16[1280]{0:T(1024)(128)(2,1)S(1)}) all-reduce(bf16[1280]{0:T(1024)(128)(2,1)S(1)} %dynamic-update-slice, bf16[1280]{0:T(1024)(128)(2,1)S(1)} %dynamic-update-slice.1), channel_id=1, replica_groups=mesh['ctx'=8,'fsdp'=16] {'ctx','fsdp'}, use_global_device_ids=true, to_apply=%add | all-reduce | flops 2560 | bytes 10240
  83.8 188.3 %all-gather.1 = bf16[128,10,320]{2,1,0:T(8,128)(2,1)} all-gather(bf16[1,10,320]{2,1,0:T(8,128)(2,1)} %bitcast.254), channel_id=1, replica_groups=mesh['ctx'=8,'fsdp'=16] {'ctx','fsdp'}, dimensions={0}, use_global_device_ids=true | all-gather | bytes 825600 | tf_op jit(solution)/shard_map/all_gather | solution.py:136
  272.1 2.4 reshape.281
  276.0 27.3 %all_gather.42 = bf16[1024,320]{0,1:T(8,128)(2,1)S(1)} all-gather(bf16[128,320]{0,1:T(8,128)(2,1)S(1)} %bitcast.248), channel_id=1, replica_groups=mesh['ctx'=8,'fsdp'=16] {'ctx'}, dimensions={0}, use_global_device_ids=true | all-gather | bytes 737280 | tf_op jit(solution)/shard_map/all_gather | solution.py:160
  303.3 189.2 %all-gather.2 = bf16[128,10,320]{2,1,0:T(8,128)(2,1)} all-gather(bf16[1,10,320]{2,1,0:T(8,128)(2,1)S(1)} %bitcast.255), channel_id=1, replica_groups=mesh['ctx'=8,'fsdp'=16] {'ctx','fsdp'}, dimensions={0}, use_global_device_ids=true | all-gather | bytes 825600 | tf_op jit(solution)/shard_map/all_gather | solution.py:137
  492.6 3.2 reshape.283
  497.5 29.6 %all_gather.44 = bf16[1024,320]{0,1:T(8,128)(2,1)} all-gather(bf16[128,320]{0,1:T(8,128)(2,1)S(1)} %convolution_convert_fusion.5), channel_id=1, replica_groups=mesh['ctx'=8,'fsdp'=16] {'ctx'}, dimensions={0}, use_global_device_ids=true | all-gather | bytes 737280 | tf_op jit(solution)/shard_map/all_gather | solution.py:161
  527.1 7.0 reshape.279
  534.1 3.3 fusion.95
  537.6 15.7 %while.30 = (s32[]{:T(128)}, bf16[5,4,128,64]{2,3,1,0:T(8,128)(2,1)S(1)}, f32[5,4,128]{2,1,0:T(4,128)S(1)}, bf16[5,4,128,64]{2,3,1,0:T(8,128)(2,1)S(1)}, bf16[5,...) while((s32[]{:T(128)}, ...), condition=%wide.region_5.6_spmd.clone.clone, body=%wide.region_2.5_spmd.clone.sunk.clone | while | flops 141164032 | bytes 7298801 | solution.py:172
  553.4 7.2 reshape.285
  560.6 2.8 multiply_reduce_fusion.1
  564.5 1.8 fusion.69
  566.4 4.1 all_to_all.60
  570.5 2.8 copy.60
  573.2 4.3 all-to-all-start.1
  577.5 4.1 all_to_all.56
  581.6 2.8 copy.59
  584.4 11.2 all-to-all-done.1
  595.6 4.3 all-to-all-start
  599.9 2.2 reshape.291
  602.1 38.6 %all-gather.15.cloned.1.call-done = bf16[1024,1280]{1,0:T(8,128)(2,1)} async-done(((bf16[128,1280]{1,0:T(8,128)(2,1)}), bf16[1024,1280]{1,0:T(8,128)(2,1)}) %all-gather.15.cloned.1.call-update) | async-done | bytes 2621456 | tf_op jit(solution)/shard_map/all_gather | solution.py:191
  640.7 4.7 fusion.101
  645.5 4.8 fusion.100
  650.3 48.6 %all-gather.17.cloned.1.call-done = bf16[1024,1280]{1,0:T(8,128)(2,1)} async-done(((bf16[128,1280]{1,0:T(8,128)(2,1)}), bf16[1024,1280]{1,0:T(8,128)(2,1)}) %all-gather.17.cloned.1.call-update) | async-done | bytes 2621456 | tf_op jit(solution)/shard_map/all_gather | solution.py:215
  698.9 6.5 multiply_convert_fusion.1
  706.3 3.1 convolution_convert_fusion
  709.7 3.3 fusion.102
  713.1 4.5 add_convert_fusion
  717.7 68.1 %reduce-scatter.11.cloned.1.call-done = bf16[128,1280]{1,0:T(8,128)(2,1)} async-done(((bf16[1024,1280]{1,0:T(8,128)(2,1)}), bf16[128,1280]{1,0:T(8,128)(2,1)}) %reduce-scatter.11.cloned.1.call-update) | async-done | bytes 327696 | tf_op jit(solution)/shard_map/reduce_scatter | solution.py:195
  785.8 80.6 %reduce-scatter.13.cloned.1.call-done = bf16[128,1280]{1,0:T(8,128)(2,1)} async-done(((bf16[1024,1280]{1,0:T(8,128)(2,1)}), bf16[128,1280]{1,0:T(8,128)(2,1)}) %reduce-scatter.13.cloned.1.call-update) | async-done | bytes 327696 | tf_op jit(solution)/shard_map/reduce_scatter | solution.py:223
  866.4 3.0 fusion.64
  871.1 37.4 %while.31 = (s32[]{:T(128)}, f32[5,4,128,64]{2,3,1,0:T(8,128)}, bf16[5,1024,64]{1,2,0:T(8,128)(2,1)}, bf16[5,1024,64]{1,2,0:T(8,128)(2,1)}, bf16[5,4,128,64]{2,3...) while((s32[]{:T(128)}, f32[5,4,128,64]{2,3,1,0:T(8,128)}, ...), condition=%wide.region_12.13_spmd.clone.clone, body=%wide.region_10.12_spmd.clone.sunk.clone | while | flops 341016064 | bytes 17322760 | solution.py:269
  883.2 1.8 fusion.190
  890.7 1.8 fusion.190
  898.2 1.8 fusion.190
  905.6 1.8 fusion.190
  908.5 2.3 copy.67
  910.9 4.1 convolution_convert_fusion.2
  915.0 2.5 copy.62
  917.5 4.4 all-to-all-start.2
  923.2 4.1 convolution_convert_fusion.1
  927.3 2.4 copy.64
  929.7 11.7 all-to-all-done.2
  941.4 4.3 all-to-all-start.3
  946.0 3.1 copy.63
  949.1 3.5 all_to_all.67
  952.7 10.4 all-to-all-done.3
  963.1 3.1 copy.65
  966.2 3.6 all_to_all.71
  970.1 3.9 fusion.90
  974.0 3.8 fusion.71
  977.7 15.6 %reduce-scatter.15.cloned.1.call-done = bf16[128,320]{1,0:T(8,128)(2,1)} async-done(((bf16[1024,320]{1,0:T(8,128)(2,1)}), bf16[128,320]{1,0:T(8,128)(2,1)}) %reduce-scatter.15.cloned.1.call-update) | async-done | bytes 81936
  996.3 71.7 %reduce-scatter.17.cloned.1.call-done = bf16[128,320]{1,0:T(8,128)(2,1)} async-done(((bf16[1024,320]{1,0:T(8,128)(2,1)}), bf16[128,320]{1,0:T(8,128)(2,1)}) %reduce-scatter.17.cloned.1.call-update) | async-done | bytes 81936
  1067.9 2.7 fusion.86
  1071.8 4.1 convolution_convert_fusion.3
  1075.9 39.5 %fusion.4 = bf16[32,1280]{1,0:T(8,128)(2,1)S(1)} fusion(bf16[448,1280]{1,0:T(8,128)(2,1)} %convolution_convert_fusion.3), kind=kCustom, calls=%all-reduce-scatter | all-reduce-scatter fusion | flops 655361 | bytes 1229312
  1115.4 4.3 collective-permute-start
  1124.2 2.0 pad_maximum_fusion.3
  1126.2 70.6 %all-reduce.21.cloned.1.call-done = (bf16[160,3584]{1,0:T(8,128)(2,1)}, bf16[160,3584]{1,0:T(8,128)(2,1)}) async-done(((bf16[160,3584]{1,0:T(8,128)(2,1)}, bf16[160,3584]{1,0:T(8,128)(2,1)}), (bf16[160,3584]{1,0:T(8,128)(2,1)}, bf16[160,3584]{1,0:T(8,128)(2,1)})) %all-reduce.21.cloned.1.call-update) | async-done | bytes 2293776
  1196.8 1.8 dynamic-slice_convert_fusion
  1198.6 20.5 %psum.7 = f32[3]{0:T(128)S(1)} all-reduce(f32[3]{0:T(128)S(1)} %pad_maximum_fusion.3), channel_id=1, replica_groups=mesh['ctx'=8,'fsdp'=16] {'ctx'}, use_global_device_ids=true, to_apply=%region_30.31 | all-reduce | flops 3 | bytes 24 | tf_op jit(solution)/shard_map/psum | solution.py:210
  1223.2 66.9 %all-reduce.12 = (f32[1280]{0:T(1024)S(1)}, f32[1280]{0:T(1024)S(1)}) all-reduce(f32[1280]{0:T(1024)S(1)} %get-tuple-element.169, f32[1280]{0:T(1024)S(1)} %copy-done.17), channel_id=6, replica_groups=mesh['ctx'=8,'fsdp'=16] {'ctx','fsdp'}, use_global_device_ids=true, to_apply=%region_17.18.clone | all-reduce | flops 2560 | bytes 20480
  1292.2 131.5 %all-reduce.19.cloned.1.call-done = (f32[1280,1280]{1,0:T(8,128)}, f32[1280,320]{1,0:T(8,128)}, f32[1280,320]{1,0:T(8,128)}, f32[1280,1280]{1,0:T(8,128)}) async-done(((f32[1280,1280]{1,0:T(8,128)}, f32[1280,320]{1,0:T(8,128)}, f32[1280,320]{1,0:T(8,128)}, f32[1280,1280]{1,0:T(8,128)}), (f32[1280,1280]{1,0:T(8,128)}, f32[1280,320]{1,0:T(8,128)}, f32[1280,320]{1,0:T(8,128)}, ...) | async-done | bytes 16384016
  (198 shorter events, 77.4 us)
Async XLA Ops:
  7.2 519.9 %all-gather.19.cloned.1.call-start = ((), (), s32[]{:S(2)}) async-start(), calls=%async_computation.12 | async-start | bytes 5283840 | tf_op jit(solution)/shard_map/all_gather | solution.py:135
  7.9 545.4 %all-gather.21.cloned.1.call-start = ((), (), s32[]{:S(2)}) async-start(), calls=%async_computation.13 | async-start | bytes 5283840 | tf_op jit(solution)/shard_map/all_gather | solution.py:138
  8.7 557.7 %all-gather.25.cloned.1.call-start = ((), (), s32[]{:S(2)}) async-start(), calls=%async_computation.15 | async-start | bytes 1949696 | tf_op jit(solution)/shard_map/all_gather | solution.py:184
  9.4 568.1 %all-gather.23.cloned.1.call-start = ((), (), s32[]{:S(2)}) async-start(), calls=%async_computation.14 | async-start | bytes 1949696 | tf_op jit(solution)/shard_map/all_gather | solution.py:183
  10.0 589.9 %all-gather.27.cloned.1.call-start = ((), (), s32[]{:S(2)}) async-start(), calls=%async_computation.16 | async-start | bytes 1392640 | tf_op jit(solution)/shard_map/all_gather | solution.py:185
  10.6 630.2 %all-gather.15.cloned.1.call-start = ((), (), s32[]{:S(2)}) async-start(), calls=%async_computation.8 | async-start | bytes 2949120 | tf_op jit(solution)/shard_map/all_gather | solution.py:191
  14.0 260.5 %copy-start.20 = (s32[1,8]{1,0:T(1,128)S(1)}, s32[1,8]{1,0:T(1,128)}, u32[]{:S(2)}) copy-start(s32[1,8]{1,0:T(1,128)} %param.28) | copy-start | bytes 100
  83.8 191.7 %copy-start = (bf16[128,1280]{1,0:T(8,128)(2,1)S(1)}, bf16[128,1280]{1,0:T(8,128)(2,1)}, u32[]{:S(2)}) copy-start(bf16[128,1280]{1,0:T(8,128)(2,1)} %param.18) | copy-start | bytes 983044
  272.1 31.3 %copy-start.18 = (bf16[10,320]{1,0:T(8,128)(2,1)S(1)}, bf16[10,320]{1,0:T(8,128)(2,1)}, u32[]{:S(2)}) copy-start(bf16[10,320]{1,0:T(8,128)(2,1)} %param.22) | copy-start | bytes 19204
  275.5 262.0 %copy-start.13 = (f32[128,32]{0,1:T(8,128)}, f32[128,32]{0,1:T(8,128)S(1)}, u32[]{:S(2)}) copy-start(f32[128,32]{0,1:T(8,128)S(1)} %get-tuple-element.259) | copy-start | bytes 49156
  553.3 7.3 copy-start.3
  553.3 7.3 copy-start.4
  564.3 134.6 %all-gather.17.cloned.1.call-start = ((), (), s32[]{:S(2)}) async-start(), calls=%async_computation.10 | async-start | bytes 2949120 | tf_op jit(solution)/shard_map/all_gather | solution.py:215
  573.2 22.3 %all-to-all-start.1 = ((bf16[160,8,448]{2,0,1:T(8,128)(2,1)}), bf16[160,8,448]{2,0,1:T(8,128)(2,1)}, u32[]{:S(2)}, u32[]{:S(2)}) async-start(bf16[160,8,448]{2,0,1:T(8,128)(2,1)} %copy.60), calls=%async_computation.1 | async-start | bytes 2621440 | tf_op jit(solution)/shard_map/all_to_all | solution.py:189
  595.6 49.9 %all-to-all-start = ((bf16[160,8,448]{2,0,1:T(8,128)(2,1)}), bf16[160,8,448]{2,0,1:T(8,128)(2,1)}, u32[]{:S(2)}, u32[]{:S(2)}) async-start(bf16[160,8,448]{2,0,1:T(8,128)(2,1)} %copy.59), calls=%async_computation | async-start | bytes 2621440 | tf_op jit(solution)/shard_map/all_to_all | solution.py:188
  599.8 185.9 %reduce-scatter.11.cloned.1.call-start = ((), (), s32[]{:S(2)}) async-start(), calls=%async_computation.9 | async-start | bytes 2949120 | tf_op jit(solution)/shard_map/reduce_scatter | solution.py:195
  698.9 7.4 copy-start.8
  705.4 1.0 copy-start.22
  709.5 156.9 %reduce-scatter.13.cloned.1.call-start = ((), (), s32[]{:S(2)}) async-start(), calls=%async_computation.11 | async-start | bytes 2949120 | tf_op jit(solution)/shard_map/reduce_scatter | solution.py:223
  709.7 3.3 copy-start.9
  717.6 275.8 %reduce-scatter.15.cloned.1.call-start = ((), (), s32[]{:S(2)}) async-start(), calls=%async_computation.17 | async-start | bytes 884736
  866.4 3.0 copy-start.6
  866.4 3.0 copy-start.7
  866.4 3.3 copy-start.2
  908.5 2.4 copy-start.21
  915.0 6.9 copy-start.11
  917.5 5.7 copy-start.10
  917.5 23.9 %all-to-all-start.2 = ((bf16[8,160,448]{2,1,0:T(8,128)(2,1)}), bf16[8,160,448]{2,1,0:T(8,128)(2,1)}, u32[]{:S(2)}, u32[]{:S(2)}) async-start(bf16[8,160,448]{2,1,0:T(8,128)(2,1)} %bitcast.230), calls=%async_computation.4 | async-start | bytes 2621440 | tf_op jit(solution)/shard_map/all_to_all | solution.py:233
  921.9 146.0 %reduce-scatter.17.cloned.1.call-start = ((), (), s32[]{:S(2)}) async-start(), calls=%async_computation.18 | async-start | bytes 884736
  941.4 21.7 %all-to-all-start.3 = ((bf16[8,160,448]{2,1,0:T(8,128)(2,1)}), bf16[8,160,448]{2,1,0:T(8,128)(2,1)}, u32[]{:S(2)}, u32[]{:S(2)}) async-start(bf16[8,160,448]{2,1,0:T(8,128)(2,1)} %bitcast.231), calls=%async_computation.5 | async-start | bytes 2621440 | tf_op jit(solution)/shard_map/all_to_all | solution.py:236
  945.7 251.1 %all-reduce.21.cloned.1.call-start = ((), (), s32[]{:S(2)}) async-start(), calls=%async_computation.20 | async-start | bytes 4587520
  966.2 3.7 copy-start.12
  966.2 3.7 copy-start.14
  966.2 3.7 copy-start.16
  969.9 453.8 %all-reduce.19.cloned.1.call-start = ((), (), s32[]{:S(2)}) async-start(), calls=%async_computation.19 | async-start | bytes 34078720
  970.1 3.9 copy-start.5
  1070.6 1.2 copy-start.23
  1071.8 49.3 %copy-start.19 = (u32[128]{0:T(128)S(1)}, u32[128]{0:T(128)}, u32[]{:S(2)}) copy-start(u32[128]{0:T(128)} %constant.170) | copy-start | bytes 1540
  1075.9 144.2 %copy-start.15 = (bf16[128,320]{1,0:T(8,128)(2,1)S(1)}, bf16[128,320]{1,0:T(8,128)(2,1)}, u32[]{:S(2)}) copy-start(bf16[128,320]{1,0:T(8,128)(2,1)} %reduce-scatter.17.cloned.1.call-done) | copy-start | bytes 245764
  1115.4 7.6 collective-permute-start
  1119.8 3.2 collective-permute-start.1
  1219.1 2.6 copy-start.1
  1221.7 1.4 copy-start.17
Sparse Core Ops, SparseCore 0:
  9.7 203.3 all-gather.18
  214.8 202.4 all-gather.20
  419.1 32.9 all-gather.24
  453.6 33.9 all-gather.22
  489.2 34.5 all-gather.26
  564.4 76.2 all-gather.14
  643.0 55.8 all-gather.16
  709.6 76.1 reduce-scatter.10
  789.6 76.7 reduce-scatter.12
  911.0 82.3 reduce-scatter.14
  997.0 70.8 reduce-scatter.16
  1070.4 126.3 all-reduce.20
  1203.1 220.5 all-reduce.18
where the time goes:
time: 1440 us; the launch traced here: 1430 us
  blocking collectives  630 us (44%)
  waiting for transfers between devices  562 us (39%)
  matrix products  111 us (8%)
  local copies, waits for them, and re-layouts  68 us (5%)
  starting transfers between devices  24 us (2%)
  other arithmetic  21 us (1%)
  between operations  17.5 us (1%)
    unnamed x19, waiting for transfers between devices  293 us
    all_gather x1, blocking collectives, local(): lax.all_gather(w_value, ('ctx', 'fsdp'), axis=0, tiled=True)  189 us
    all_gather x1, blocking collectives, local(): lax.all_gather(w_key, ('ctx', 'fsdp'), axis=0, tiled=True)  188 us
    unnamed x3, blocking collectives  175 us
    reduce_scatter x1, waiting for transfers between devices, local(): lax.psum_scatter((jnp.einsum('rf,df->rd', gate_low, gate_part, preferred_...  80.6 us
    reduce_scatter x1, waiting for transfers between devices, local(): lax.psum_scatter(jnp.dot(hidden, down_part, preferred_element_type=jnp.fl...  68.1 us
    all_gather x1, waiting for transfers between devices, local(): grad_rows = lax.all_gather(feed_grad, 'ctx', axis=0, tiled=True)  48.6 us
    all_gather x1, waiting for transfers between devices, local(): normed_rows = lax.all_gather(normed_two, 'ctx', axis=0, tiled=True)  38.6 us
  transfers between devices with their start and end apart: 19, of which 11 were waited for; matrix products, arithmetic and copies ran while one was open for 11% of the time, Pallas kernels for 0%

commit v1 on v0

v1 whole, which is shorter than its diff:
```python
import jax
import jax.numpy as jnp
from jax import lax
from jax.sharding import Mesh, PartitionSpec as P

QUERY_HEADS = 20
KEY_VALUE_HEADS = 5
HEAD_WIDTH = 64
QUERY_WIDTH = QUERY_HEADS * HEAD_WIDTH
KEY_WIDTH = KEY_VALUE_HEADS * HEAD_WIDTH
GAIN_COLS = 128
PAD_UNITS = 32

EPSILON = 1e-05
ROPE_BASE = 10000.0
MASKED_SCORE = -1e30

AXES = ("y", "zh", "x", "zl", "core")
SIZES = (4, 2, 4, 2, 2)
ROW_AXES = ("y", "core")
SLICE_AXES = ("x", "zh", "zl")
F32 = jnp.float32
BF16 = jnp.bfloat16


def device_number(x, y, z, core):
    return (((y * 2 + z // 2) * 4 + x) * 2 + z % 2) * 2 + core


def pairs_of(move):
    pairs = []
    for y in range(4):
        for z in range(4):
            for x in range(4):
                for core in range(2):
                    tx, ty, tz, tc = move(x, y, z, core)
                    pairs.append(
                        (device_number(x, y, z, core), device_number(tx % 4, ty % 4, tz % 4, tc))
                    )
    return pairs


def send(values, move):
    return lax.ppermute(values, AXES, pairs_of(move))


def swap_cores(values):
    return send(values, lambda x, y, z, core: (x, y, z, 1 - core))


def swap_half_core(values):
    return send(values, lambda x, y, z, core: (x, y, core * 2 + z % 2, z // 2))


def stage_move(stage, distance):
    def move(x, y, z, core):
        spot = [x, y, z]
        spot[(stage + core) % 3] += distance
        return (spot[0], spot[1], spot[2], core)

    return move


def gather_stage(values, stage):
    arrived = [send(values, stage_move(stage, -distance)) for distance in (1, 2, 3)]
    return jnp.concatenate([values] + arrived, axis=0)


def reduce_stage(values, stage):
    rows = values.shape[0] // 4
    parts = [values[step * rows : (step + 1) * rows] for step in range(4)]
    total = parts[0].astype(F32)
    for distance in (1, 2, 3):
        total = total + send(parts[distance], stage_move(stage, distance)).astype(F32)
    return total


def reduce_rows(term):
    low = term.astype(BF16)
    half = low.shape[0] // 2
    total = low[:half].astype(F32) + swap_cores(low[half:]).astype(F32)
    for stage in (2, 1, 0):
        total = reduce_stage(total.astype(BF16), stage)
    return total


def row_order(place, core):
    x, y, z = place
    third, second, first, inner = jnp.meshgrid(
        jnp.arange(4), jnp.arange(4), jnp.arange(4), jnp.arange(10), indexing="ij"
    )
    if core == 0:
        sx, sy, sz = x + first, y + second, z + third
    else:
        sy, sz, sx = y + first, z + second, x + third
    numbers = device_number(sx % 4, sy % 4, sz % 4, core) * 10 + inner
    return numbers.reshape(-1).astype(jnp.int32)


def slice_order():
    x, zh, zl, y, core, inner = jnp.meshgrid(
        *(jnp.arange(n) for n in (4, 2, 2, 4, 2, 10)), indexing="ij"
    )
    return (device_number(x, y, zh * 2 + zl, core) * 10 + inner).reshape(-1).astype(jnp.int32)


def one_hot(order):
    return (jnp.arange(order.shape[0], dtype=jnp.int32)[:, None] == order[None, :]).astype(BF16)


def exact_move(values, hot):
    high = values.astype(BF16)
    low = (values - high.astype(F32)).astype(BF16)
    return mm(high, hot) + mm(low, hot)


def mm(left, right):
    return jnp.dot(left, right, preferred_element_type=F32)


def mm_nt(left, right):
    return lax.dot_general(left, right, (((1,), (1,)), ((), ())), preferred_element_type=F32)


def mm_tn(left, right):
    return lax.dot_general(left, right, (((0,), (0,)), ((), ())), preferred_element_type=F32)


def norm_factor(values):
    return lax.rsqrt(jnp.mean(values * values, axis=-1, keepdims=True) + EPSILON)


def norm_back(values, factor, gain, grad):
    weighted = gain * grad
    inner = jnp.mean(weighted * values, axis=-1, keepdims=True)
    return factor * weighted - values * (factor * factor * factor) * inner


def rope_tables(angles_at, head_size):
    half_size = head_size // 2
    powers = jnp.arange(half_size, dtype=F32) * (2.0 / head_size)
    speeds = jnp.power(ROPE_BASE, -powers)
    angles = angles_at[:, None] * speeds[None, :]
    return (jnp.cos(angles)[:, None, :], jnp.sin(angles)[:, None, :])


def apply_rotary(values, cosine_values, sine_values):
    half_size = values.shape[-1] // 2
    leading = values[..., :half_size]
    trailing = values[..., half_size:]
    return jnp.concatenate(
        [
            leading * cosine_values - trailing * sine_values,
            trailing * cosine_values + leading * sine_values,
        ],
        axis=-1,
    )


def group_places(pair_row, devices_ctx, block_size):
    slots = jnp.arange(devices_ctx * 2 * block_size, dtype=jnp.int32)
    owners = slots // (2 * block_size)
    inside = slots % (2 * block_size)
    columns = jnp.arange(devices_ctx, dtype=jnp.int32)
    paired = jnp.sum(jnp.where(owners[:, None] == columns[None, :], pair_row[None, :], 0), axis=1)
    blocks = jnp.where(inside < block_size, paired, 2 * devices_ctx - 1 - paired)
    return blocks * block_size + inside % block_size


def head_scores(query_head, key_head, allowed, scale_factor):
    scores = (
        jnp.einsum("grd,kd->grk", query_head, key_head, preferred_element_type=F32) * scale_factor
    )
    return jnp.where(allowed[None], scores, MASKED_SCORE)


def head_forward(query_head, key_head, value_head, allowed, scale_factor):
    scores = head_scores(query_head, key_head, allowed, scale_factor)
    row_top = jnp.max(scores, axis=-1, keepdims=True)
    expons = jnp.exp(scores - row_top)
    totals = jnp.sum(expons, axis=-1, keepdims=True)
    chances = (expons / totals).astype(BF16)
    outcome = jnp.einsum("grk,kd->grd", chances, value_head, preferred_element_type=F32)
    return (outcome, row_top[..., 0] + jnp.log(totals[..., 0]))


def head_backward(query_head, key_head, value_head, grad_head, log_totals, allowed, scale_factor):
    scores = head_scores(query_head, key_head, allowed, scale_factor)
    chances = jnp.exp(scores - log_totals[..., None])
    chances_low = chances.astype(BF16)
    chance_grad = jnp.einsum("grd,kd->grk", grad_head, value_head, preferred_element_type=F32)
    weighted = jnp.sum(chances * chance_grad, axis=-1, keepdims=True)
    score_grad = (chances * (chance_grad - weighted)).astype(BF16)
    query_grad = (
        jnp.einsum("grk,kd->grd", score_grad, key_head, preferred_element_type=F32) * scale_factor
    )
    key_grad = (
        jnp.einsum("grk,grd->kd", score_grad, query_head, preferred_element_type=F32)
        * scale_factor
    )
    value_grad = jnp.einsum("grk,grd->kd", chances_low, grad_head, preferred_element_type=F32)
    return (query_grad, key_grad, value_grad)


def pack_units(weight):
    rows = weight.shape[0]
    runs = weight.reshape(rows, 8, 4, 2, 2, 28).transpose(1, 0, 2, 4, 3, 5)
    runs = jnp.pad(runs, ((0, 0),) * 5 + ((0, PAD_UNITS - 28),))
    return runs.reshape(8, rows, 16 * PAD_UNITS)


def unpack_units(packed):
    rows = packed.shape[1]
    runs = packed.reshape(8, rows, 4, 2, 2, PAD_UNITS)[..., :28]
    return runs.transpose(1, 0, 2, 4, 3, 5).reshape(rows, 8 * 16 * 28)


def local(
    tokens,
    norm_gain,
    w_query,
    w_key,
    w_value,
    w_out,
    mlp_gain,
    w_gate,
    w_up,
    w_down,
    block_pair,
    seq_len,
    seq_start,
    out_grad,
):
    shard_rows, model_width = tokens.shape
    block_size = shard_rows // 2
    devices_ctx = 8
    at_y, at_zh, at_x, at_zl, at_core = (lax.axis_index(name) for name in AXES)
    place = (at_x, at_y, at_zh * 2 + at_zl)
    position = at_y * 2 + at_zh
    query_per_key = QUERY_HEADS // KEY_VALUE_HEADS
    scale_factor = HEAD_WIDTH ** (-0.5)

    gains = jnp.stack([norm_gain, mlp_gain], axis=1)
    gains = jnp.pad(gains, ((0, 0), (0, GAIN_COLS - 2)))
    packed = jnp.concatenate([w_key, w_value, gains, w_query, w_out], axis=1)
    packed = gather_stage(packed, 0)
    packed = gather_stage(packed, 1)
    split = 2 * KEY_WIDTH + GAIN_COLS
    key_part = gather_stage(packed[:, :split], 2)
    key_other = swap_cores(key_part)
    query_part = gather_stage(packed[:, split : split + QUERY_WIDTH], 2)
    query_other = swap_cores(query_part)
    out_part = gather_stage(packed[:, split + QUERY_WIDTH :], 2)
    out_other = swap_cores(out_part)

    units = jnp.concatenate([pack_units(w_gate), pack_units(w_up)], axis=2)
    units = lax.all_to_all(units, ROW_AXES, 0, 0, tiled=True)
    units_full = lax.all_gather(
        units.reshape(-1, units.shape[2]), SLICE_AXES, axis=0, tiled=True
    )
    down_rows = swap_half_core(jnp.pad(w_down, ((0, PAD_UNITS - w_down.shape[0]), (0, 0))))
    down_full = lax.all_gather(down_rows, SLICE_AXES, axis=0, tiled=True)

    places_all = group_places(block_pair[0], devices_ctx, block_size)
    places_here = lax.dynamic_slice_in_dim(places_all, position * shard_rows, shard_rows)
    first_slot = seq_start[0]
    seq_length = seq_len[0]
    valid_all = (places_all >= first_slot) & (places_all < first_slot + seq_length)
    valid_here = (places_here >= first_slot) & (places_here < first_slot + seq_length)
    allowed = valid_here[:, None] & valid_all[None, :] & (
        places_all[None, :] <= places_here[:, None]
    ) | (places_all[None, :] == places_here[:, None])
    cosine, sine = rope_tables((places_here - first_slot).astype(F32), HEAD_WIDTH)
    row_weight = valid_here.astype(F32)[:, None]

    orders = [row_order(place, core) for core in (0, 1)]
    mine = jnp.where(at_core == 0, orders[0], orders[1])
    other = jnp.where(at_core == 0, orders[1], orders[0])
    hot = one_hot(jnp.concatenate([mine, other]))
    half = model_width // 2
    slice_hot = one_hot(slice_order())

    cotangent = out_grad.astype(F32) * row_weight
    feed_grad = cotangent.astype(BF16)
    grad_rows = lax.all_gather(feed_grad, ROW_AXES, axis=0, tiled=True)

    inputs = tokens.astype(F32)
    factor_one = norm_factor(inputs)
    tokens_moved = mm(tokens, hot)
    gain_cols = jnp.concatenate([key_part[:, 2 * KEY_WIDTH :], key_other[:, 2 * KEY_WIDTH :]])
    gain_rows = gain_cols.T[:8]
    gain_one = gain_rows[0:1].astype(F32)
    gain_two = mm_nt(gain_rows, hot)[1:2]
    normed = (tokens_moved * factor_one * gain_one).astype(BF16)

    def project(rows, part, other_part):
        return mm(rows[:, :half], part) + mm(rows[:, half:], other_part)

    key_value = project(normed, key_part[:, : 2 * KEY_WIDTH], key_other[:, : 2 * KEY_WIDTH])
    keys = apply_rotary(
        key_value[:, :KEY_WIDTH].reshape(shard_rows, KEY_VALUE_HEADS, HEAD_WIDTH), cosine, sine
    ).reshape(shard_rows, KEY_WIDTH)
    low_pairs = jnp.concatenate([keys, key_value[:, KEY_WIDTH:]], axis=1).astype(BF16)
    gathered = lax.all_to_all(
        jnp.broadcast_to(low_pairs[None], (devices_ctx,) + low_pairs.shape),
        ("y", "zh"),
        0,
        0,
        tiled=True,
    ).reshape(devices_ctx * shard_rows, 2 * KEY_WIDTH)

    query_pre = project(normed, query_part, query_other)
    queries = apply_rotary(
        query_pre.reshape(shard_rows, QUERY_HEADS, HEAD_WIDTH), cosine, sine
    ).astype(BF16)
    query_heads = queries.reshape(
        shard_rows, KEY_VALUE_HEADS, query_per_key, HEAD_WIDTH
    ).transpose(1, 2, 0, 3)
    key_heads = (
        gathered[:, :KEY_WIDTH].reshape(-1, KEY_VALUE_HEADS, HEAD_WIDTH).transpose(1, 0, 2)
    )
    value_heads = (
        gathered[:, KEY_WIDTH:].reshape(-1, KEY_VALUE_HEADS, HEAD_WIDTH).transpose(1, 0, 2)
    )

    def forward_head(pieces):
        return head_forward(pieces[0], pieces[1], pieces[2], allowed, scale_factor)

    head_outs, log_totals = lax.map(forward_head, (query_heads, key_heads, value_heads))
    attended = (
        head_outs.transpose(2, 0, 1, 3).reshape(shard_rows, QUERY_WIDTH).astype(BF16)
    )
    attended_moved = mm(attended, hot).astype(BF16)
    branch = project(attended_moved, out_part, out_other)
    middle = inputs + branch
    factor_two = norm_factor(middle)
    normed_two = (middle * factor_two * gain_two).astype(BF16)
    normed_two = mm(normed_two, slice_hot).astype(BF16)

    normed_rows = lax.all_gather(normed_two, ROW_AXES, axis=0, tiled=True)
    gate_up = mm(normed_rows, units_full)
    units_here = gate_up.shape[1] // 2
    gate_value = gate_up[:, :units_here]
    up_value = gate_up[:, units_here:]
    gate_sigmoid = 1.0 / (1.0 + jnp.exp(-gate_value))
    gate_silu = gate_value * gate_sigmoid
    hidden = (gate_silu * up_value).astype(BF16)
    hidden_grad = mm_nt(grad_rows, down_full)
    gate_low = hidden_grad * up_value * gate_sigmoid * (1.0 + gate_value * (1.0 - gate_sigmoid))
    up_low = hidden_grad * gate_silu
    unit_grads = jnp.concatenate([gate_low.astype(BF16), up_low.astype(BF16)], axis=1)
    normed_two_grad = lax.psum_scatter(
        mm_nt(unit_grads, units_full).astype(BF16), ROW_AXES, scatter_dimension=0, tiled=True
    ).astype(F32)
    feed_out = lax.psum_scatter(
        mm(hidden, down_full).astype(BF16), ROW_AXES, scatter_dimension=0, tiled=True
    ).astype(F32)
    unit_term = lax.psum_scatter(
        mm_tn(normed_rows, unit_grads).astype(BF16), SLICE_AXES, scatter_dimension=0, tiled=True
    )
    down_term = lax.psum_scatter(
        mm_tn(hidden, grad_rows).astype(BF16), SLICE_AXES, scatter_dimension=0, tiled=True
    )
    final_out = middle + feed_out
    sums = jnp.stack(
        [
            jnp.sum(row_weight * branch * branch),
            jnp.sum(row_weight * feed_out * feed_out),
            jnp.sum(row_weight * final_out * final_out),
        ]
    )
    sums = jnp.broadcast_to(jnp.pad(sums, (0, 125))[None], (8, 128))
    sums = sums + send(sums, lambda x, y, z, core: (x, y, z + 2, core))
    sums = sums + send(sums, lambda x, y, z, core: (x, y ^ 1, z, core))
    sums = sums + send(sums, lambda x, y, z, core: (x, y ^ 2, z, core))
    seq_rms = jnp.sqrt(sums[:1, :3] / (seq_length.astype(F32) * model_width))

    normed_two_grad = exact_move(normed_two_grad, slice_hot.T)
    mid_grad = cotangent + norm_back(middle, factor_two, gain_two, normed_two_grad)
    gain_two_rows = mm((normed_two_grad * middle * factor_two).astype(BF16), hot).astype(BF16)
    branch_grad = mid_grad.astype(BF16)
    attended_grad = jnp.concatenate(
        [mm_nt(branch_grad, out_part), mm_nt(branch_grad, out_other)], axis=1
    ).astype(BF16)
    attended_grad = mm_nt(attended_grad, hot).astype(BF16)
    out_sum = reduce_rows(mm_tn(attended_moved, branch_grad))
    grad_heads = attended_grad.reshape(
        shard_rows, KEY_VALUE_HEADS, query_per_key, HEAD_WIDTH
    ).transpose(1, 2, 0, 3)

    def backward_head(pieces):
        return head_backward(
            pieces[0], pieces[1], pieces[2], pieces[3], pieces[4], allowed, scale_factor
        )

    query_parts, key_pieces, value_pieces = lax.map(
        backward_head, (query_heads, key_heads, value_heads, grad_heads, log_totals)
    )
    query_grad = query_parts.transpose(2, 0, 1, 3).reshape(shard_rows, QUERY_HEADS, HEAD_WIDTH)
    pair_grads = jnp.concatenate(
        [
            key_pieces.transpose(1, 0, 2).reshape(-1, KEY_WIDTH),
            value_pieces.transpose(1, 0, 2).reshape(-1, KEY_WIDTH),
        ],
        axis=1,
    ).astype(BF16)
    pair_grads = lax.all_to_all(
        pair_grads.reshape(devices_ctx, shard_rows, 2 * KEY_WIDTH), ("y", "zh"), 0, 0, tiled=True
    )
    pair_grads = jnp.sum(pair_grads.astype(F32), axis=0)
    query_low = (
        apply_rotary(query_grad, cosine, -sine).reshape(shard_rows, QUERY_WIDTH).astype(BF16)
    )
    key_grad = apply_rotary(
        pair_grads[:, :KEY_WIDTH].reshape(shard_rows, KEY_VALUE_HEADS, HEAD_WIDTH), cosine, -sine
    ).reshape(shard_rows, KEY_WIDTH)
    pair_low = jnp.concatenate([key_grad, pair_grads[:, KEY_WIDTH:]], axis=1).astype(BF16)
    query_sum = reduce_rows(mm_tn(normed, query_low))

    def project_back(grads, part, other_part):
        return jnp.concatenate([mm_nt(grads, part), mm_nt(grads, other_part)], axis=1)

    normed_grad = project_back(query_low, query_part, query_other) + project_back(
        pair_low, key_part[:, : 2 * KEY_WIDTH], key_other[:, : 2 * KEY_WIDTH]
    )
    input_part = norm_back(tokens_moved, factor_one, gain_one, normed_grad)
    input_grad = (mid_grad + exact_move(input_part, hot.T)).astype(BF16)
    gain_one_rows = (normed_grad * tokens_moved * factor_one).astype(BF16)
    picks = jnp.arange(GAIN_COLS) < GAIN_COLS // 2
    picks = jnp.broadcast_to(picks[None], (shard_rows, GAIN_COLS))
    gain_terms = mm_tn(gain_one_rows, picks.astype(BF16)) + mm_tn(
        gain_two_rows, (~picks).astype(BF16)
    )
    pair_sum = reduce_rows(
        jnp.concatenate([mm_tn(normed, pair_low), gain_terms], axis=1)
    )

    unit_term = lax.all_to_all(
        unit_term.reshape(8, -1, unit_term.shape[1]), ROW_AXES, 0, 0, tiled=True
    ).astype(F32)
    down_sum = swap_half_core(down_term)[: w_down.shape[0]].astype(F32)
    return (
        final_out.astype(BF16),
        input_grad,
        pair_sum[:, 2 * KEY_WIDTH],
        query_sum,
        pair_sum[:, :KEY_WIDTH],
        pair_sum[:, KEY_WIDTH : 2 * KEY_WIDTH],
        out_sum,
        pair_sum[:, 2 * KEY_WIDTH + GAIN_COLS - 1],
        unpack_units(unit_term[:, :, :units_here]),
        unpack_units(unit_term[:, :, units_here:]),
        down_sum,
        seq_rms,
    )


def solution(mesh):
    fine = Mesh(mesh.devices.reshape(SIZES), AXES)
    rows = P(AXES, None)
    flat = P(AXES)
    group = ("x", "zl", "core")
    in_specs = (
        (rows, flat, rows, rows, rows, rows, flat, rows, rows, rows)
        + (P(group, None), P(group), P(group))
        + (rows,)
    )
    out_specs = (rows, rows, flat, rows, rows, rows, rows, flat, rows, rows, rows, P(group, None))
    return jax.shard_map(
        local, mesh=fine, in_specs=in_specs, out_specs=out_specs, check_vma=False
    )
```

time: 1440 us -> 638 us (0.44)
  the two profiles are of different devices: /device:TPU:1 before, /device:TPU:0 now
where the time goes in v1:
time: 638 us; the launch traced here: 627 us
  waiting for transfers between devices  286 us (45%)
  matrix products  136 us (21%)
  starting transfers between devices  98.2 us (15%)
  local copies, waits for them, and re-layouts  50.6 us (8%)
  other arithmetic  37.9 us (6%)
  between operations  17.5 us (3%)
    ppermute x53, starting transfers between devices, send(): return lax.ppermute(values, AXES, pairs_of(move))  79.9 us
    reduce_scatter x1, waiting for transfers between devices, local(): lax.psum_scatter(mm_tn(hidden, grad_rows).astype(BF16), SLICE_AXES, scatt...  61.1 us
    ppermute x53, waiting for transfers between devices, send(): return lax.ppermute(values, AXES, pairs_of(move))  46.1 us
    all_gather x1, waiting for transfers between devices, local(): down_full = lax.all_gather(down_rows, SLICE_AXES, axis=0, tiled=True)  39.3 us
    dot_general x15, matrix products, mm(): return jnp.dot(left, right, preferred_element_type=F32)  36.1 us
    reduce_scatter x1, waiting for transfers between devices, local(): lax.psum_scatter(mm(hidden, down_full).astype(BF16), ROW_AXES, scatter_di...  31.1 us
    all_gather x1, waiting for transfers between devices, local(): grad_rows = lax.all_gather(feed_grad, ROW_AXES, axis=0, tiled=True)  27.7 us
    reduce_scatter x1, waiting for transfers between devices, local(): lax.psum_scatter(mm_nt(unit_grads, units_full).astype(BF16), ROW_AXES, sc...  26.8 us
  transfers between devices with their start and end apart: 65, of which 27 were waited for; matrix products, arithmetic and copies ran while one was open for 33% of the time, Pallas kernels for 0%

profile of v1, /device:TPU:0, one launch (start us, length us, event | category | flops | bytes accessed | tf_op | source)
XLA Modules:
  0.0 627.1 jit_solution(578670624087428553)
XLA Ops:
  8.9 2.9 collective-permute-start
  18.7 4.5 all-to-all-start.1
  27.3 3.2 collective-permute-start.3
  33.8 3.5 collective-permute-done.3
  38.6 2.7 collective-permute-done.5
  43.3 4.1 collective-permute-start.6
  49.5 4.3 collective-permute-done.6
  55.2 2.2 collective-permute-done.8
  61.9 2.7 collective-permute-start.14
  70.1 2.5 collective-permute-done.12
  82.9 4.3 all-to-all-start
  97.9 10.1 %all-to-all-done = bf16[8,128,640]{1,2,0:T(8,128)(2,1)} async-done(((bf16[8,128,640]{1,2,0:T(8,128)(2,1)}), bf16[8,128,640]{1,2,0:T(8,128)(2,1)}, u32[]{:S(2)}, u32[]{:S(2)}) %all-to-all-start) | async-done | bytes 1310752 | tf_op jit(solution)/shard_map/all_to_all | solution.py:304
  108.0 2.5 copy.147
  110.5 2.9 fusion.189
  113.4 2.3 copy.148
  115.7 2.3 copy.149
  118.0 26.2 %while.30 = (s32[]{:T(128)}, bf16[5,4,128,64]{2,3,1,0:T(8,128)(2,1)}, f32[5,4,128]{2,1,0:T(4,128)}, bf16[5,4,128,64]{2,3,1,0:T(8,128)(2,1)}, bf16[5,1024,64]{1,2...) while((s32[]{:T(128)}, ...), condition=%wide.region_5.6_spmd.clone.clone, body=%wide.region_2.5_spmd.clone.sunk.clone | while | flops 141164032 | bytes 7299301 | solution.py:329
  121.0 2.3 fusion.270
  126.2 2.3 fusion.270
  131.5 2.3 fusion.270
  136.7 2.3 fusion.270
  141.9 2.3 fusion.270
  144.2 2.5 fusion.77
  150.9 2.2 fusion.80
  156.8 20.9 %all-gather.5.cloned.1.call-done = bf16[1024,1280]{1,0:T(8,128)(2,1)} async-done(((bf16[128,1280]{1,0:T(8,128)(2,1)}), bf16[1024,1280]{1,0:T(8,128)(2,1)}) %all-gather.5.cloned.1.call-update) | async-done | bytes 2621456 | tf_op jit(solution)/shard_map/all_gather | solution.py:340
  177.7 7.5 %fusion.200 = f32[1024,1024]{0,1:T(8,128)} fusion(bf16[1024,1280]{1,0:T(8,128)(2,1)} %all-gather.5.cloned.1.call-done, bf16[1280,1024]{1,0:T(8,128)(2,1)} %all-gather.7.cloned.1.call-done), kind=kOutput, calls=%fused_computation.373 | convolution fusion | flops 2684354560 | bytes 9437184 | tf_op jit(solution)/shard_map/dot_general | solution.py:118
  185.2 39.3 %all-gather.9.cloned.1.call-done = bf16[512,1280]{1,0:T(8,128)(2,1)} async-done(((bf16[32,1280]{1,0:T(8,128)(2,1)}), bf16[512,1280]{1,0:T(8,128)(2,1)}) %all-gather.9.cloned.1.call-update) | async-done | bytes 1310736 | tf_op jit(solution)/shard_map/all_gather | solution.py:262
  224.5 27.7 %all-gather.11.cloned.1.call-done = bf16[1024,1280]{1,0:T(8,128)(2,1)} async-done(((bf16[128,1280]{1,0:T(8,128)(2,1)}), bf16[1024,1280]{1,0:T(8,128)(2,1)}) %all-gather.11.cloned.1.call-update) | async-done | bytes 2621456 | tf_op jit(solution)/shard_map/all_gather | solution.py:285
  252.2 7.1 %multiply_convert_fusion.2 = (bf16[1024,512]{0,1:T(8,128)(2,1)}, bf16[1024,512]{0,1:T(8,128)(2,1)}, bf16[1024,512]{0,1:T(8,128)(2,1)S(1)}) fusion(f32[1024,1024]{0,1:T(8,128)} %fusion.200, bf16[1024,1280]{1,0:T(8,128)(2,1)} %all-gather.11.cloned.1.call-done, bf16[512,1280]{1,0:T(8,128)(2,1)} %all-gather.9.cloned.1.call-done), kind=kOutput, calls=%fused_computation.107 | convolution fusion | flops 1350041600 | bytes 11272192 | tf_op jit(solution)/shard_map/dot_general | solution.py:122
  260.3 2.6 convolution_convert_fusion.6
  263.0 6.8 %convolution_convert_fusion.4 = bf16[1024,1280]{1,0:T(8,128)(2,1)} fusion(bf16[1280,1024]{1,0:T(8,128)(2,1)} %all-gather.7.cloned.1.call-done, bf16[1024,512]{0,1:T(8,128)(2,1)} %get-tuple-element.318, bf16[1024,512]{0,1:T(8,128)(2,1)} %get-tuple-element.317), kind=kOutput, calls=%fused_computation.75 | convolution fusion | flops 2689859584 | bytes 7340032 | tf_op jit(solution)/shard_map/dot_general | solution.py:122
  269.9 4.7 convolution_convert_fusion.2
  275.9 61.1 %reduce-scatter.11.cloned.1.call-done = bf16[32,1280]{1,0:T(8,128)(2,1)} async-done(((bf16[512,1280]{1,0:T(8,128)(2,1)}), bf16[32,1280]{1,0:T(8,128)(2,1)}) %reduce-scatter.11.cloned.1.call-update) | async-done | bytes 81936 | tf_op jit(solution)/shard_map/reduce_scatter | solution.py:361
  339.0 6.8 %convolution_convert_fusion.3 = bf16[1280,1024]{1,0:T(8,128)(2,1)} fusion(bf16[1024,1280]{1,0:T(8,128)(2,1)} %all-gather.5.cloned.1.call-done, bf16[1024,512]{0,1:T(8,128)(2,1)} %get-tuple-element.318, bf16[1024,512]{0,1:T(8,128)(2,1)} %get-tuple-element.317), kind=kOutput, calls=%fused_computation.74 | convolution fusion | flops 2689859584 | bytes 7340032 | tf_op jit(solution)/shard_map/dot_general | solution.py:126
  346.5 26.8 %reduce-scatter.7.cloned.1.call-done = bf16[128,1280]{1,0:T(8,128)(2,1)} async-done(((bf16[1024,1280]{1,0:T(8,128)(2,1)}), bf16[128,1280]{1,0:T(8,128)(2,1)}) %reduce-scatter.7.cloned.1.call-update) | async-done | bytes 327696 | tf_op jit(solution)/shard_map/reduce_scatter | solution.py:352
  373.3 2.5 fusion.47
  375.8 2.3 fusion.71
  378.1 31.1 %reduce-scatter.5.cloned.1.call-done = bf16[128,1280]{1,0:T(8,128)(2,1)} async-done(((bf16[1024,1280]{1,0:T(8,128)(2,1)}), bf16[128,1280]{1,0:T(8,128)(2,1)}) %reduce-scatter.5.cloned.1.call-update) | async-done | bytes 327696 | tf_op jit(solution)/shard_map/reduce_scatter | solution.py:355
  409.3 3.3 fusion.94
  415.2 3.3 collective-permute-start.50
  423.5 42.7 %while.31 = (s32[]{:T(128)}, f32[5,4,128,64]{2,3,1,0:T(8,128)S(1)}, bf16[5,1024,64]{1,2,0:T(8,128)(2,1)}, bf16[5,1024,64]{1,2,0:T(8,128)(2,1)}, bf16[5,4,128,64]...) while((s32[]{:T(128)}, f32[5,4,128,64]{2,3,1,0:T(8,128)S(1)}, ...), condition=%wide.region_12.13_spmd.clone.clone, body=%wide.region_10.12_spmd.clone.sunk.clone | while | flops 341016064 | bytes 17322752 | solution.py:396
  466.4 2.7 convolution_convert_fusion.1
  469.2 2.8 convolution_convert_fusion
  473.3 13.5 %reduce-scatter.9.cloned.1.call-done = bf16[80,1024]{1,0:T(8,128)(2,1)} async-done(((bf16[1280,1024]{1,0:T(8,128)(2,1)}), bf16[80,1024]{1,0:T(8,128)(2,1)}) %reduce-scatter.9.cloned.1.call-update) | async-done | bytes 163856 | tf_op jit(solution)/shard_map/reduce_scatter | solution.py:358
  488.4 4.3 all-to-all-start.3
  492.7 2.7 slice.399
  502.8 3.2 collective-permute-start.52
  506.0 4.6 all-to-all-start.2
  518.8 9.7 %all-to-all-done.2 = bf16[8,128,640]{1,2,0:T(8,128)(2,1)S(1)} async-done(((bf16[8,128,640]{1,2,0:T(8,128)(2,1)}), bf16[8,128,640]{1,2,0:T(8,128)(2,1)S(1)}, u32[]{:S(2)}, u32[]{:S(2)}) %all-to-all-start.2) | async-done | bytes 1310752 | tf_op jit(solution)/shard_map/all_to_all | solution.py:407
  533.0 2.8 fusion.75
  538.5 2.3 fusion.76
  543.8 2.6 collective-permute-start.41
  553.1 3.8 collective-permute-done.41
  558.3 3.8 collective-permute-done.30
  562.1 7.2 %collective-permute-start.44 = (bf16[40,1280]{1,0:T(8,128)(2,1)S(1)}, bf16[40,1280]{1,0:T(8,128)(2,1)S(1)}, u32[]{:S(2)}, u32[]{:S(2)}) collective-permute-start(bf16[40,1280]{1,0:T(8,128)(2,1)S(1)} %get-tuple-element.340), channel_id=1, source_target_pairs={{0,64},{1,17},{4,68},{5,21},{8,72},{9,25},{12,76},{13,29},{2,66},{... | collective-permute-start | bytes 307208 | tf_op jit(solution)/shard_map/ppermute | solution.py:44
  572.4 2.8 collective-permute-start.35
  575.2 2.9 collective-permute-start.21
  580.4 3.4 collective-permute-start.47
  583.9 4.5 collective-permute-done.20
  595.1 2.5 collective-permute-start.25
  598.3 4.5 collective-permute-done.23
  602.8 4.7 collective-permute-start.38
  607.9 2.5 collective-permute-start.27
  611.8 5.1 collective-permute-done.26
  (463 shorter events, 183.1 us)
Async XLA Ops:
  8.9 18.2 %collective-permute-start = (bf16[10,3328]{1,0:T(8,128)(2,1)S(1)}, bf16[10,3328]{1,0:T(8,128)(2,1)S(1)}, u32[]{:S(2)}, u32[]{:S(2)}) collective-permute-start(bf16[10,3328]{1,0:T(8,128)(2,1)S(1)} %concatenate.90), channel_id=1, source_target_pairs={{0,12},{1,97},{4,0},{5,101},{8,4},{9,105},{12,8},{13,109},{2,14},{... | collective-permute-start | bytes 199688 | tf_op jit(solution)/shard_map/ppermute | solution.py:44
  11.9 15.3 %collective-permute-start.1 = (bf16[10,3328]{1,0:T(8,128)(2,1)S(1)}, bf16[10,3328]{1,0:T(8,128)(2,1)S(1)}, u32[]{:S(2)}, u32[]{:S(2)}) collective-permute-start(bf16[10,3328]{1,0:T(8,128)(2,1)S(1)} %concatenate.90), channel_id=1, source_target_pairs={{0,8},{1,65},{4,12},{5,69},{8,0},{9,73},{12,4},{13,77},{2,10},{3,6... | collective-permute-start | bytes 199688 | tf_op jit(solution)/shard_map/ppermute | solution.py:44
  12.7 14.6 %collective-permute-start.2 = (bf16[10,3328]{1,0:T(8,128)(2,1)S(1)}, bf16[10,3328]{1,0:T(8,128)(2,1)S(1)}, u32[]{:S(2)}, u32[]{:S(2)}) collective-permute-start(bf16[10,3328]{1,0:T(8,128)(2,1)S(1)} %concatenate.90), channel_id=1, source_target_pairs={{0,4},{1,33},{4,8},{5,37},{8,12},{9,41},{12,0},{13,45},{2,6},{3,35... | collective-permute-start | bytes 199688 | tf_op jit(solution)/shard_map/ppermute | solution.py:44
  18.7 42.5 %all-to-all-start.1 = ((bf16[8,10,1024]{2,1,0:T(8,128)(2,1)}), bf16[8,10,1024]{2,1,0:T(8,128)(2,1)S(1)}, u32[]{:S(2)}, u32[]{:S(2)}) async-start(bf16[8,10,1024]{2,1,0:T(8,128)(2,1)} %copy.152), calls=%async_computation.1 | async-start | bytes 524288 | tf_op jit(solution)/shard_map/all_to_all | solution.py:257
  23.2 133.6 %all-gather.7.cloned.1.call-start = ((), (), s32[]{:S(2)}) async-start(), calls=%async_computation.9 | async-start | bytes 2785280 | tf_op jit(solution)/shard_map/all_gather | solution.py:258
  27.3 10.0 %collective-permute-start.3 = (bf16[40,3328]{1,0:T(8,128)(2,1)S(1)}, bf16[40,3328]{1,0:T(8,128)(2,1)S(1)}, u32[]{:S(2)}, u32[]{:S(2)}) collective-permute-start(bf16[40,3328]{1,0:T(8,128)(2,1)S(1)} %pad_maximum_fusion.9), channel_id=1, source_target_pairs={{0,96},{1,19},{4,100},{5,23},{8,104},{9,27},{12,108},{13,31},{2,98... | collective-permute-start | bytes 798728 | tf_op jit(solution)/shard_map/ppermute | solution.py:44
  30.6 8.0 %collective-permute-start.4 = (bf16[40,3328]{1,0:T(8,128)(2,1)S(1)}, bf16[40,3328]{1,0:T(8,128)(2,1)S(1)}, u32[]{:S(2)}, u32[]{:S(2)}) collective-permute-start(bf16[40,3328]{1,0:T(8,128)(2,1)S(1)} %pad_maximum_fusion.9), channel_id=1, source_target_pairs={{0,64},{1,17},{4,68},{5,21},{8,72},{9,25},{12,76},{13,29},{2,66},{... | collective-permute-start | bytes 798728 | tf_op jit(solution)/shard_map/ppermute | solution.py:44
  31.4 9.9 %collective-permute-start.5 = (bf16[40,3328]{1,0:T(8,128)(2,1)S(1)}, bf16[40,3328]{1,0:T(8,128)(2,1)S(1)}, u32[]{:S(2)}, u32[]{:S(2)}) collective-permute-start(bf16[40,3328]{1,0:T(8,128)(2,1)S(1)} %pad_maximum_fusion.9), channel_id=1, source_target_pairs={{0,32},{1,3},{4,36},{5,7},{8,40},{9,11},{12,44},{13,15},{2,34},{3,... | collective-permute-start | bytes 798728 | tf_op jit(solution)/shard_map/ppermute | solution.py:44
  43.3 10.5 %collective-permute-start.6 = (bf16[160,768]{1,0:T(8,128)(2,1)S(1)}, bf16[160,768]{1,0:T(8,128)(2,1)S(1)}, u32[]{:S(2)}, u32[]{:S(2)}) collective-permute-start(bf16[160,768]{1,0:T(8,128)(2,1)S(1)} %slice.338), channel_id=1, source_target_pairs={{0,18},{1,13},{4,22},{5,1},{8,26},{9,5},{12,30},{13,9},{2,0},{3,15... | collective-permute-start | bytes 737288 | tf_op jit(solution)/shard_map/ppermute | solution.py:44
  47.4 7.8 %collective-permute-start.7 = (bf16[160,768]{1,0:T(8,128)(2,1)S(1)}, bf16[160,768]{1,0:T(8,128)(2,1)S(1)}, u32[]{:S(2)}, u32[]{:S(2)}) collective-permute-start(bf16[160,768]{1,0:T(8,128)(2,1)S(1)} %slice.338), channel_id=1, source_target_pairs={{0,16},{1,9},{4,20},{5,13},{8,24},{9,1},{12,28},{13,5},{2,18},{3,1... | collective-permute-start | bytes 737288 | tf_op jit(solution)/shard_map/ppermute | solution.py:44
  47.4 10.0 %collective-permute-start.8 = (bf16[160,768]{1,0:T(8,128)(2,1)S(1)}, bf16[160,768]{1,0:T(8,128)(2,1)S(1)}, u32[]{:S(2)}, u32[]{:S(2)}) collective-permute-start(bf16[160,768]{1,0:T(8,128)(2,1)S(1)} %slice.338), channel_id=1, source_target_pairs={{0,2},{1,5},{4,6},{5,9},{8,10},{9,13},{12,14},{13,1},{2,16},{3,7},... | collective-permute-start | bytes 737288 | tf_op jit(solution)/shard_map/ppermute | solution.py:44
  57.6 17.8 %collective-permute-start.9 = (bf16[640,768]{1,0:T(8,128)(2,1)S(1)}, bf16[640,768]{1,0:T(8,128)(2,1)}, u32[]{:S(2)}, u32[]{:S(2)}) collective-permute-start(bf16[640,768]{1,0:T(8,128)(2,1)S(1)} %pad_maximum_fusion.7), channel_id=1, source_target_pairs={{0,1},{1,0},{4,5},{5,4},{8,9},{9,8},{12,13},{13,12},{2,3},{3,2},{6... | collective-permute-start | bytes 2949128 | tf_op jit(solution)/shard_map/ppermute | solution.py:44
  57.7 8.0 %collective-permute-start.10 = (bf16[160,1280]{1,0:T(8,128)(2,1)S(1)}, bf16[160,1280]{1,0:T(8,128)(2,1)S(1)}, u32[]{:S(2)}, u32[]{:S(2)}) collective-permute-start(bf16[160,1280]{1,0:T(8,128)(2,1)S(1)} %get-tuple-element.328), channel_id=1, source_target_pairs={{0,18},{1,13},{4,22},{5,1},{8,26},{9,5},{12,30},{13,9},{2,0},{3,15... | collective-permute-start | bytes 1228808 | tf_op jit(solution)/shard_map/ppermute | solution.py:44
  58.7 9.6 %collective-permute-start.11 = (bf16[160,1280]{1,0:T(8,128)(2,1)S(1)}, bf16[160,1280]{1,0:T(8,128)(2,1)S(1)}, u32[]{:S(2)}, u32[]{:S(2)}) collective-permute-start(bf16[160,1280]{1,0:T(8,128)(2,1)S(1)} %get-tuple-element.328), channel_id=1, source_target_pairs={{0,16},{1,9},{4,20},{5,13},{8,24},{9,1},{12,28},{13,5},{2,18},{3,1... | collective-permute-start | bytes 1228808 | tf_op jit(solution)/shard_map/ppermute | solution.py:44
  58.7 13.9 %collective-permute-start.12 = (bf16[160,1280]{1,0:T(8,128)(2,1)S(1)}, bf16[160,1280]{1,0:T(8,128)(2,1)}, u32[]{:S(2)}, u32[]{:S(2)}) collective-permute-start(bf16[160,1280]{1,0:T(8,128)(2,1)S(1)} %get-tuple-element.328), channel_id=1, source_target_pairs={{0,2},{1,5},{4,6},{5,9},{8,10},{9,13},{12,14},{13,1},{2,16},{3,7},... | collective-permute-start | bytes 1228808 | tf_op jit(solution)/shard_map/ppermute | solution.py:44
  61.9 25.4 %collective-permute-start.14 = (bf16[160,1280]{1,0:T(8,128)(2,1)S(1)}, bf16[160,1280]{1,0:T(8,128)(2,1)}, u32[]{:S(2)}, u32[]{:S(2)}) collective-permute-start(bf16[160,1280]{1,0:T(8,128)(2,1)S(1)} %get-tuple-element.329), channel_id=1, source_target_pairs={{0,18},{1,13},{4,22},{5,1},{8,26},{9,5},{12,30},{13,9},{2,0},{3,15... | collective-permute-start | bytes 1228808 | tf_op jit(solution)/shard_map/ppermute | solution.py:44
  65.8 21.6 %collective-permute-start.15 = (bf16[160,1280]{1,0:T(8,128)(2,1)S(1)}, bf16[160,1280]{1,0:T(8,128)(2,1)}, u32[]{:S(2)}, u32[]{:S(2)}) collective-permute-start(bf16[160,1280]{1,0:T(8,128)(2,1)S(1)} %get-tuple-element.329), channel_id=1, source_target_pairs={{0,16},{1,9},{4,20},{5,13},{8,24},{9,1},{12,28},{13,5},{2,18},{3,1... | collective-permute-start | bytes 1228808 | tf_op jit(solution)/shard_map/ppermute | solution.py:44
  68.3 19.1 %collective-permute-start.16 = (bf16[160,1280]{1,0:T(8,128)(2,1)S(1)}, bf16[160,1280]{1,0:T(8,128)(2,1)}, u32[]{:S(2)}, u32[]{:S(2)}) collective-permute-start(bf16[160,1280]{1,0:T(8,128)(2,1)S(1)} %get-tuple-element.329), channel_id=1, source_target_pairs={{0,2},{1,5},{4,6},{5,9},{8,10},{9,13},{12,14},{13,1},{2,16},{3,7},... | collective-permute-start | bytes 1228808 | tf_op jit(solution)/shard_map/ppermute | solution.py:44
  74.0 16.5 %collective-permute-start.13 = (bf16[640,1280]{1,0:T(8,128)(2,1)S(1)}, bf16[640,1280]{1,0:T(8,128)(2,1)}, u32[]{:S(2)}, u32[]{:S(2)}) collective-permute-start(bf16[640,1280]{1,0:T(8,128)(2,1)S(1)} %pad_maximum_fusion.1), channel_id=1, source_target_pairs={{0,1},{1,0},{4,5},{5,4},{8,9},{9,8},{12,13},{13,12},{2,3},{3,2},{6... | collective-permute-start | bytes 4915208 | tf_op jit(solution)/shard_map/ppermute | solution.py:44
  82.9 25.1 %all-to-all-start = ((bf16[8,128,640]{1,2,0:T(8,128)(2,1)}), bf16[8,128,640]{1,2,0:T(8,128)(2,1)}, u32[]{:S(2)}, u32[]{:S(2)}) async-start(bf16[8,128,640]{1,2,0:T(8,128)(2,1)} %broadcast_in_dim.232), calls=%async_computation | async-start | bytes 2621440 | tf_op jit(solution)/shard_map/all_to_all | solution.py:304
  87.2 90.5 %all-gather.5.cloned.1.call-start = ((), (), s32[]{:S(2)}) async-start(), calls=%async_computation.8 | async-start | bytes 2949120 | tf_op jit(solution)/shard_map/all_gather | solution.py:340
  88.9 57.8 %collective-permute-start.17 = (bf16[640,1280]{1,0:T(8,128)(2,1)S(1)}, bf16[640,1280]{1,0:T(8,128)(2,1)}, u32[]{:S(2)}, u32[]{:S(2)}) collective-permute-start(bf16[640,1280]{1,0:T(8,128)(2,1)S(1)} %pad_maximum_fusion.2), channel_id=1, source_target_pairs={{0,1},{1,0},{4,5},{5,4},{8,9},{9,8},{12,13},{13,12},{2,3},{3,2},{6... | collective-permute-start | bytes 4915208 | tf_op jit(solution)/shard_map/ppermute | solution.py:44
  153.2 71.3 %all-gather.9.cloned.1.call-start = ((), (), s32[]{:S(2)}) async-start(), calls=%async_computation.10 | async-start | bytes 1392640 | tf_op jit(solution)/shard_map/all_gather | solution.py:262
  154.6 97.6 %all-gather.11.cloned.1.call-start = ((), (), s32[]{:S(2)}) async-start(), calls=%async_computation.12 | async-start | bytes 2949120 | tf_op jit(solution)/shard_map/all_gather | solution.py:285
  156.5 180.5 %reduce-scatter.11.cloned.1.call-start = ((), (), s32[]{:S(2)}) async-start(), calls=%async_computation.15 | async-start | bytes 1392640 | tf_op jit(solution)/shard_map/reduce_scatter | solution.py:361
  262.9 110.3 %reduce-scatter.7.cloned.1.call-start = ((), (), s32[]{:S(2)}) async-start(), calls=%async_computation.13 | async-start | bytes 2949120 | tf_op jit(solution)/shard_map/reduce_scatter | solution.py:352
  269.9 139.4 %reduce-scatter.5.cloned.1.call-start = ((), (), s32[]{:S(2)}) async-start(), calls=%async_computation.11 | async-start | bytes 2949120 | tf_op jit(solution)/shard_map/reduce_scatter | solution.py:355
  274.7 212.1 %reduce-scatter.9.cloned.1.call-start = ((), (), s32[]{:S(2)}) async-start(), calls=%async_computation.14 | async-start | bytes 2785280 | tf_op jit(solution)/shard_map/reduce_scatter | solution.py:358
  337.0 8.8 %collective-permute-start.49 = (bf16[32,1280]{1,0:T(8,128)(2,1)}, bf16[32,1280]{1,0:T(8,128)(2,1)S(1)}, u32[]{:S(2)}, u32[]{:S(2)}) collective-permute-start(bf16[32,1280]{1,0:T(8,128)(2,1)} %reduce-scatter.11.cloned.1.call-done), channel_id=1, source_target_pairs={{0,0},{1,16},{4,4},{5,20},{8,8},{9,24},{12,12},{13,28},{2,2},{3,18... | collective-permute-start | bytes 245768 | tf_op jit(solution)/shard_map/ppermute | solution.py:44
  415.2 82.2 %collective-permute-start.50 = (f32[8,128]{1,0:T(8,128)}, f32[8,128]{1,0:T(8,128)}, u32[]{:S(2)}, u32[]{:S(2)}) collective-permute-start(f32[8,128]{1,0:T(8,128)} %broadcast_in_dim.245), channel_id=1, source_target_pairs={{0,16},{1,17},{4,20},{5,21},{8,24},{9,25},{12,28},{13,29},{2,18},{... | collective-permute-start | bytes 12296 | tf_op jit(solution)/shard_map/ppermute | solution.py:44
  488.4 17.6 %all-to-all-start.3 = ((bf16[8,10,1024]{2,1,0:T(8,128)(2,1)}), bf16[8,10,1024]{2,1,0:T(8,128)(2,1)S(1)}, u32[]{:S(2)}, u32[]{:S(2)}) async-start(bf16[8,10,1024]{2,1,0:T(8,128)(2,1)} %reshape.420), calls=%async_computation.6 | async-start | bytes 524288 | tf_op jit(solution)/shard_map/all_to_all | solution.py:438
  495.4 45.5 %collective-permute-start.39 = (bf16[640,1280]{1,0:T(8,128)(2,1)}, bf16[640,1280]{1,0:T(8,128)(2,1)}, u32[]{:S(2)}, u32[]{:S(2)}) collective-permute-start(bf16[640,1280]{1,0:T(8,128)(2,1)} %slice.399), channel_id=1, source_target_pairs={{0,1},{1,0},{4,5},{5,4},{8,9},{9,8},{12,13},{13,12},{2,3},{3,2},{6... | collective-permute-start | bytes 4915208 | tf_op jit(solution)/shard_map/ppermute | solution.py:44
  497.2 50.8 %collective-permute-start.29 = (bf16[640,1280]{1,0:T(8,128)(2,1)}, bf16[640,1280]{1,0:T(8,128)(2,1)}, u32[]{:S(2)}, u32[]{:S(2)}) collective-permute-start(bf16[640,1280]{1,0:T(8,128)(2,1)} %slice.383), channel_id=1, source_target_pairs={{0,1},{1,0},{4,5},{5,4},{8,9},{9,8},{12,13},{13,12},{2,3},{3,2},{6... | collective-permute-start | bytes 4915208 | tf_op jit(solution)/shard_map/ppermute | solution.py:44
  498.5 3.6 collective-permute-start.51
  502.8 9.9 %collective-permute-start.52 = (f32[8,128]{1,0:T(8,128)S(1)}, f32[8,128]{1,0:T(8,128)S(1)}, u32[]{:S(2)}, u32[]{:S(2)}) collective-permute-start(f32[8,128]{1,0:T(8,128)S(1)} %fusion.232), channel_id=1, source_target_pairs={{0,64},{1,65},{4,68},{5,69},{8,72},{9,73},{12,76},{13,77},{2,66},{... | collective-permute-start | bytes 12296 | tf_op jit(solution)/shard_map/ppermute | solution.py:44
  506.0 22.6 %all-to-all-start.2 = ((bf16[8,128,640]{1,2,0:T(8,128)(2,1)}), bf16[8,128,640]{1,2,0:T(8,128)(2,1)S(1)}, u32[]{:S(2)}, u32[]{:S(2)}) async-start(bf16[8,128,640]{1,2,0:T(8,128)(2,1)} %copy.156), calls=%async_computation.4 | async-start | bytes 2621440 | tf_op jit(solution)/shard_map/all_to_all | solution.py:407
  536.0 35.6 %collective-permute-start.19 = (bf16[640,768]{0,1:T(8,128)(2,1)S(1)}, bf16[640,768]{0,1:T(8,128)(2,1)S(1)}, u32[]{:S(2)}, u32[]{:S(2)}) collective-permute-start(bf16[640,768]{0,1:T(8,128)(2,1)S(1)} %pad_maximum_fusion.6), channel_id=1, source_target_pairs={{0,1},{1,0},{4,5},{5,4},{8,9},{9,8},{12,13},{13,12},{2,3},{3,2},{6... | collective-permute-start | bytes 2949128 | tf_op jit(solution)/shard_map/ppermute | solution.py:44
  543.0 9.2 %collective-permute-start.40 = (bf16[160,1280]{1,0:T(8,128)(2,1)S(1)}, bf16[160,1280]{1,0:T(8,128)(2,1)S(1)}, u32[]{:S(2)}, u32[]{:S(2)}) collective-permute-start(bf16[160,1280]{1,0:T(8,128)(2,1)S(1)} %get-tuple-element.320), channel_id=1, source_target_pairs={{0,2},{1,5},{4,6},{5,9},{8,10},{9,13},{12,14},{13,1},{2,16},{3,7},... | collective-permute-start | bytes 1228808 | tf_op jit(solution)/shard_map/ppermute | solution.py:44
  543.8 13.1 %collective-permute-start.41 = (bf16[160,1280]{1,0:T(8,128)(2,1)S(1)}, bf16[160,1280]{1,0:T(8,128)(2,1)S(1)}, u32[]{:S(2)}, u32[]{:S(2)}) collective-permute-start(bf16[160,1280]{1,0:T(8,128)(2,1)S(1)} %get-tuple-element.322), channel_id=1, source_target_pairs={{0,16},{1,9},{4,20},{5,13},{8,24},{9,1},{12,28},{13,5},{2,18},{3,1... | collective-permute-start | bytes 1228808 | tf_op jit(solution)/shard_map/ppermute | solution.py:44
  546.4 11.1 %collective-permute-start.42 = (bf16[160,1280]{1,0:T(8,128)(2,1)S(1)}, bf16[160,1280]{1,0:T(8,128)(2,1)S(1)}, u32[]{:S(2)}, u32[]{:S(2)}) collective-permute-start(bf16[160,1280]{1,0:T(8,128)(2,1)S(1)} %get-tuple-element.321), channel_id=1, source_target_pairs={{0,18},{1,13},{4,22},{5,1},{8,26},{9,5},{12,30},{13,9},{2,0},{3,15... | collective-permute-start | bytes 1228808 | tf_op jit(solution)/shard_map/ppermute | solution.py:44
  550.0 12.1 %collective-permute-start.30 = (bf16[160,1280]{1,0:T(8,128)(2,1)S(1)}, bf16[160,1280]{1,0:T(8,128)(2,1)S(1)}, u32[]{:S(2)}, u32[]{:S(2)}) collective-permute-start(bf16[160,1280]{1,0:T(8,128)(2,1)S(1)} %get-tuple-element.323), channel_id=1, source_target_pairs={{0,2},{1,5},{4,6},{5,9},{8,10},{9,13},{12,14},{13,1},{2,16},{3,7},... | collective-permute-start | bytes 1228808 | tf_op jit(solution)/shard_map/ppermute | solution.py:44
  552.2 17.0 %collective-permute-start.31 = (bf16[160,1280]{1,0:T(8,128)(2,1)S(1)}, bf16[160,1280]{1,0:T(8,128)(2,1)S(1)}, u32[]{:S(2)}, u32[]{:S(2)}) collective-permute-start(bf16[160,1280]{1,0:T(8,128)(2,1)S(1)} %get-tuple-element.325), channel_id=1, source_target_pairs={{0,16},{1,9},{4,20},{5,13},{8,24},{9,1},{12,28},{13,5},{2,18},{3,1... | collective-permute-start | bytes 1228808 | tf_op jit(solution)/shard_map/ppermute | solution.py:44
  556.9 12.4 %collective-permute-start.32 = (bf16[160,1280]{1,0:T(8,128)(2,1)S(1)}, bf16[160,1280]{1,0:T(8,128)(2,1)S(1)}, u32[]{:S(2)}, u32[]{:S(2)}) collective-permute-start(bf16[160,1280]{1,0:T(8,128)(2,1)S(1)} %get-tuple-element.324), channel_id=1, source_target_pairs={{0,18},{1,13},{4,22},{5,1},{8,26},{9,5},{12,30},{13,9},{2,0},{3,15... | collective-permute-start | bytes 1228808 | tf_op jit(solution)/shard_map/ppermute | solution.py:44
  557.8 14.6 %collective-permute-start.43 = (bf16[40,1280]{1,0:T(8,128)(2,1)S(1)}, bf16[40,1280]{1,0:T(8,128)(2,1)S(1)}, u32[]{:S(2)}, u32[]{:S(2)}) collective-permute-start(bf16[40,1280]{1,0:T(8,128)(2,1)S(1)} %get-tuple-element.338), channel_id=1, source_target_pairs={{0,32},{1,3},{4,36},{5,7},{8,40},{9,11},{12,44},{13,15},{2,34},{3,... | collective-permute-start | bytes 307208 | tf_op jit(solution)/shard_map/ppermute | solution.py:44
  562.1 13.1 %collective-permute-start.44 = (bf16[40,1280]{1,0:T(8,128)(2,1)S(1)}, bf16[40,1280]{1,0:T(8,128)(2,1)S(1)}, u32[]{:S(2)}, u32[]{:S(2)}) collective-permute-start(bf16[40,1280]{1,0:T(8,128)(2,1)S(1)} %get-tuple-element.340), channel_id=1, source_target_pairs={{0,64},{1,17},{4,68},{5,21},{8,72},{9,25},{12,76},{13,29},{2,66},{... | collective-permute-start | bytes 307208 | tf_op jit(solution)/shard_map/ppermute | solution.py:44
  569.2 6.0 collective-permute-start.45
  569.5 8.7 %collective-permute-start.33 = (bf16[40,1280]{1,0:T(8,128)(2,1)S(1)}, bf16[40,1280]{1,0:T(8,128)(2,1)S(1)}, u32[]{:S(2)}, u32[]{:S(2)}) collective-permute-start(bf16[40,1280]{1,0:T(8,128)(2,1)S(1)} %get-tuple-element.341), channel_id=1, source_target_pairs={{0,32},{1,3},{4,36},{5,7},{8,40},{9,11},{12,44},{13,15},{2,34},{3,... | collective-permute-start | bytes 307208 | tf_op jit(solution)/shard_map/ppermute | solution.py:44
  571.6 7.0 %collective-permute-start.34 = (bf16[40,1280]{1,0:T(8,128)(2,1)S(1)}, bf16[40,1280]{1,0:T(8,128)(2,1)S(1)}, u32[]{:S(2)}, u32[]{:S(2)}) collective-permute-start(bf16[40,1280]{1,0:T(8,128)(2,1)S(1)} %get-tuple-element.343), channel_id=1, source_target_pairs={{0,64},{1,17},{4,68},{5,21},{8,72},{9,25},{12,76},{13,29},{2,66},{... | collective-permute-start | bytes 307208 | tf_op jit(solution)/shard_map/ppermute | solution.py:44
  572.4 8.0 %collective-permute-start.35 = (bf16[40,1280]{1,0:T(8,128)(2,1)S(1)}, bf16[40,1280]{1,0:T(8,128)(2,1)S(1)}, u32[]{:S(2)}, u32[]{:S(2)}) collective-permute-start(bf16[40,1280]{1,0:T(8,128)(2,1)S(1)} %get-tuple-element.342), channel_id=1, source_target_pairs={{0,96},{1,19},{4,100},{5,23},{8,104},{9,27},{12,108},{13,31},{2,98... | collective-permute-start | bytes 307208 | tf_op jit(solution)/shard_map/ppermute | solution.py:44
  575.2 13.2 %collective-permute-start.20 = (bf16[160,768]{0,1:T(8,128)(2,1)S(1)}, bf16[160,768]{0,1:T(8,128)(2,1)S(1)}, u32[]{:S(2)}, u32[]{:S(2)}) collective-permute-start(bf16[160,768]{0,1:T(8,128)(2,1)S(1)} %get-tuple-element.330), channel_id=1, source_target_pairs={{0,2},{1,5},{4,6},{5,9},{8,10},{9,13},{12,14},{13,1},{2,16},{3,7},... | collective-permute-start | bytes 737288 | tf_op jit(solution)/shard_map/ppermute | solution.py:44
  575.2 13.2 %collective-permute-start.21 = (bf16[160,768]{0,1:T(8,128)(2,1)S(1)}, bf16[160,768]{0,1:T(8,128)(2,1)S(1)}, u32[]{:S(2)}, u32[]{:S(2)}) collective-permute-start(bf16[160,768]{0,1:T(8,128)(2,1)S(1)} %get-tuple-element.332), channel_id=1, source_target_pairs={{0,16},{1,9},{4,20},{5,13},{8,24},{9,1},{12,28},{13,5},{2,18},{3,1... | collective-permute-start | bytes 737288 | tf_op jit(solution)/shard_map/ppermute | solution.py:44
  578.2 12.2 %collective-permute-start.22 = (bf16[160,768]{0,1:T(8,128)(2,1)S(1)}, bf16[160,768]{0,1:T(8,128)(2,1)S(1)}, u32[]{:S(2)}, u32[]{:S(2)}) collective-permute-start(bf16[160,768]{0,1:T(8,128)(2,1)S(1)} %get-tuple-element.331), channel_id=1, source_target_pairs={{0,18},{1,13},{4,22},{5,1},{8,26},{9,5},{12,30},{13,9},{2,0},{3,15... | collective-permute-start | bytes 737288 | tf_op jit(solution)/shard_map/ppermute | solution.py:44
  578.6 14.4 %collective-permute-start.46 = (bf16[10,1280]{1,0:T(8,128)(2,1)S(1)}, bf16[10,1280]{1,0:T(8,128)(2,1)S(1)}, u32[]{:S(2)}, u32[]{:S(2)}) collective-permute-start(bf16[10,1280]{1,0:T(8,128)(2,1)S(1)} %get-tuple-element.360), channel_id=1, source_target_pairs={{0,4},{1,33},{4,8},{5,37},{8,12},{9,41},{12,0},{13,45},{2,6},{3,35... | collective-permute-start | bytes 76808 | tf_op jit(solution)/shard_map/ppermute | solution.py:44
  580.4 13.3 %collective-permute-start.47 = (bf16[10,1280]{1,0:T(8,128)(2,1)S(1)}, bf16[10,1280]{1,0:T(8,128)(2,1)S(1)}, u32[]{:S(2)}, u32[]{:S(2)}) collective-permute-start(bf16[10,1280]{1,0:T(8,128)(2,1)S(1)} %get-tuple-element.362), channel_id=1, source_target_pairs={{0,8},{1,65},{4,12},{5,69},{8,0},{9,73},{12,4},{13,77},{2,10},{3,6... | collective-permute-start | bytes 76808 | tf_op jit(solution)/shard_map/ppermute | solution.py:44
  588.4 6.7 %collective-permute-start.48 = (bf16[10,1280]{1,0:T(8,128)(2,1)S(1)}, bf16[10,1280]{1,0:T(8,128)(2,1)S(1)}, u32[]{:S(2)}, u32[]{:S(2)}) collective-permute-start(bf16[10,1280]{1,0:T(8,128)(2,1)S(1)} %get-tuple-element.361), channel_id=1, source_target_pairs={{0,12},{1,97},{4,0},{5,101},{8,4},{9,105},{12,8},{13,109},{2,14},{... | collective-permute-start | bytes 76808 | tf_op jit(solution)/shard_map/ppermute | solution.py:44
  588.4 22.0 %collective-permute-start.36 = (bf16[10,1280]{1,0:T(8,128)(2,1)S(1)}, bf16[10,1280]{1,0:T(8,128)(2,1)S(1)}, u32[]{:S(2)}, u32[]{:S(2)}) collective-permute-start(bf16[10,1280]{1,0:T(8,128)(2,1)S(1)} %get-tuple-element.363), channel_id=1, source_target_pairs={{0,4},{1,33},{4,8},{5,37},{8,12},{9,41},{12,0},{13,45},{2,6},{3,35... | collective-permute-start | bytes 76808 | tf_op jit(solution)/shard_map/ppermute | solution.py:44
  590.4 20.7 %collective-permute-start.37 = (bf16[10,1280]{1,0:T(8,128)(2,1)S(1)}, bf16[10,1280]{1,0:T(8,128)(2,1)S(1)}, u32[]{:S(2)}, u32[]{:S(2)}) collective-permute-start(bf16[10,1280]{1,0:T(8,128)(2,1)S(1)} %get-tuple-element.365), channel_id=1, source_target_pairs={{0,8},{1,65},{4,12},{5,69},{8,0},{9,73},{12,4},{13,77},{2,10},{3,6... | collective-permute-start | bytes 76808 | tf_op jit(solution)/shard_map/ppermute | solution.py:44
  593.1 9.7 %collective-permute-start.23 = (bf16[40,768]{0,1:T(8,128)(2,1)S(1)}, bf16[40,768]{0,1:T(8,128)(2,1)S(1)}, u32[]{:S(2)}, u32[]{:S(2)}) collective-permute-start(bf16[40,768]{0,1:T(8,128)(2,1)S(1)} %get-tuple-element.348), channel_id=1, source_target_pairs={{0,32},{1,3},{4,36},{5,7},{8,40},{9,11},{12,44},{13,15},{2,34},{3,... | collective-permute-start | bytes 184328 | tf_op jit(solution)/shard_map/ppermute | solution.py:44
  593.8 13.7 %collective-permute-start.24 = (bf16[40,768]{0,1:T(8,128)(2,1)S(1)}, bf16[40,768]{0,1:T(8,128)(2,1)S(1)}, u32[]{:S(2)}, u32[]{:S(2)}) collective-permute-start(bf16[40,768]{0,1:T(8,128)(2,1)S(1)} %get-tuple-element.350), channel_id=1, source_target_pairs={{0,64},{1,17},{4,68},{5,21},{8,72},{9,25},{12,76},{13,29},{2,66},{... | collective-permute-start | bytes 184328 | tf_op jit(solution)/shard_map/ppermute | solution.py:44
  595.1 12.4 %collective-permute-start.25 = (bf16[40,768]{0,1:T(8,128)(2,1)S(1)}, bf16[40,768]{0,1:T(8,128)(2,1)S(1)}, u32[]{:S(2)}, u32[]{:S(2)}) collective-permute-start(bf16[40,768]{0,1:T(8,128)(2,1)S(1)} %get-tuple-element.349), channel_id=1, source_target_pairs={{0,96},{1,19},{4,100},{5,23},{8,104},{9,27},{12,108},{13,31},{2,98... | collective-permute-start | bytes 184328 | tf_op jit(solution)/shard_map/ppermute | solution.py:44
  602.8 8.4 %collective-permute-start.38 = (bf16[10,1280]{1,0:T(8,128)(2,1)S(1)}, bf16[10,1280]{1,0:T(8,128)(2,1)S(1)}, u32[]{:S(2)}, u32[]{:S(2)}) collective-permute-start(bf16[10,1280]{1,0:T(8,128)(2,1)S(1)} %get-tuple-element.364), channel_id=1, source_target_pairs={{0,12},{1,97},{4,0},{5,101},{8,4},{9,105},{12,8},{13,109},{2,14},{... | collective-permute-start | bytes 76808 | tf_op jit(solution)/shard_map/ppermute | solution.py:44
  607.8 9.1 %collective-permute-start.26 = (bf16[10,768]{0,1:T(8,128)(2,1)S(1)}, bf16[10,768]{0,1:T(8,128)(2,1)S(1)}, u32[]{:S(2)}, u32[]{:S(2)}) collective-permute-start(bf16[10,768]{0,1:T(8,128)(2,1)S(1)} %get-tuple-element.353), channel_id=1, source_target_pairs={{0,4},{1,33},{4,8},{5,37},{8,12},{9,41},{12,0},{13,45},{2,6},{3,35... | collective-permute-start | bytes 46088 | tf_op jit(solution)/shard_map/ppermute | solution.py:44
  607.9 9.0 %collective-permute-start.27 = (bf16[10,768]{0,1:T(8,128)(2,1)S(1)}, bf16[10,768]{0,1:T(8,128)(2,1)S(1)}, u32[]{:S(2)}, u32[]{:S(2)}) collective-permute-start(bf16[10,768]{0,1:T(8,128)(2,1)S(1)} %get-tuple-element.355), channel_id=1, source_target_pairs={{0,8},{1,65},{4,12},{5,69},{8,0},{9,73},{12,4},{13,77},{2,10},{3,6... | collective-permute-start | bytes 46088 | tf_op jit(solution)/shard_map/ppermute | solution.py:44
  610.4 7.3 %collective-permute-start.28 = (bf16[10,768]{0,1:T(8,128)(2,1)S(1)}, bf16[10,768]{0,1:T(8,128)(2,1)S(1)}, u32[]{:S(2)}, u32[]{:S(2)}) collective-permute-start(bf16[10,768]{0,1:T(8,128)(2,1)S(1)} %get-tuple-element.354), channel_id=1, source_target_pairs={{0,12},{1,97},{4,0},{5,101},{8,4},{9,105},{12,8},{13,109},{2,14},{... | collective-permute-start | bytes 46088 | tf_op jit(solution)/shard_map/ppermute | solution.py:44
  (64 other events, 705.6 us)
Sparse Core Ops, SparseCore 0:
  62.0 54.8 all-gather.6
  153.3 24.3 all-gather.4
  180.5 43.9 all-gather.8
  226.6 25.5 all-gather.10
  263.1 73.9 reduce-scatter.10
  339.3 33.9 reduce-scatter.6
  375.7 33.5 reduce-scatter.4
  412.6 74.1 reduce-scatter.8
